TPU v7x, 256 devices: a whole 4x4x8 slice. The times are simulated.
256 devices in a mesh: lon: 16 (over y_lo, x, core), lat: 8 (over z), dp: 2 (over y_hi).
Axes of the slice: x: 4, y: 4 (y_hi: 2, y_lo: 2; y = y_hi * 2 + y_lo), z: 8, core: 2. Of those that a mesh axis runs over, the one named last changes fastest.
Arguments:
- query: bfloat16 [128, 768, 512], P(('dp', 'lat'), 'lon'), parts along dimension 0, may hold values from -12 to 12
- keys: bfloat16 [128, 768, 512], P(('dp', 'lat'), 'lon'), parts along dimension 0, may hold values from -12 to 12
- values: bfloat16 [128, 768, 512], P(('dp', 'lat'), 'lon'), parts along dimension 0, may hold values from -6 to 6
- grad_out: bfloat16 [128, 768, 512], P(('dp', 'lat'), 'lon'), parts along dimension 0, may hold values from -6 to 6
- band_width: int32 [8], replicated, may hold values from 0 to 2, as said below
- cap_blocks: int32 [16], replicated, may hold values from 0 to 2, as said below
Outputs:
- attended: bfloat16 [128, 768, 512], P(('dp', 'lat'), 'lon'), parts along dimension 0
- query_grad: bfloat16 [128, 768, 512], P(('dp', 'lat'), 'lon'), parts along dimension 0
- key_grad: bfloat16 [128, 768, 512], P(('dp', 'lat'), 'lon'), parts along dimension 0
- value_grad: bfloat16 [128, 768, 512], P(('dp', 'lat'), 'lon'), parts along dimension 0
There are 2 independent parts, one for each index of `dp`. A program takes and returns all parts, laid end to end along the dimension named above; an argument that names none is the same for every part. Nothing has to cross between parts.
Inputs may be any that keep to these rules, and one draw needn't show every extreme that they name: `band_width`: both pole bands take 2; some other band takes 0. `cap_blocks`: some sector takes 0 and some takes 2.
All inputs are finite; a program needn't handle non-finite values.
Results may differ from a plain program's by a relative error of at most 0.0059.
Values may be sent and summed in bfloat16 or wider, within the bound.
No kernel may reach another device: no remote copies, remote signals or barrier semaphores. Data moves between devices by JAX's collectives and lax.ppermute only.
A program may use at most 128 MiB of HBM per device.

v0:
```python
import jax
import jax.numpy as jnp
from jax import lax
from jax.sharding import PartitionSpec as P

HEADS = 8
HSIZE = 64
BR = 8
BC = 16
HALO = 2
CR = 1
HD = 512


def padded(value, sides, width):
    for axis, dim in sides:
        peers, length = (lax.axis_size(axis), value.shape[dim])
        up = [(i, (i + 1) % peers) for i in range(peers)]
        down = [(j, i) for i, j in up]
        last = lax.slice_in_dim(value, length - width, length, axis=dim)
        leading = lax.slice_in_dim(value, 0, width, axis=dim)
        before = lax.ppermute(last, axis, up)
        after = lax.ppermute(leading, axis, down)
        value = jnp.concatenate([before, value, after], axis=dim)
    return value


def from_behind(value, axis, steps):
    count = lax.axis_size(axis)
    pairs = [(source, (source + steps) % count) for source in range(count)]
    return lax.ppermute(value, axis, pairs)


def inner_product(form, left_side, right_side):
    return jnp.einsum(form, left_side, right_side, preferred_element_type=jnp.float32)


def to_blocks(grid, block_count):
    row_count = grid.shape[0]
    feature_width = grid.shape[-1]
    split_grid = grid.reshape(row_count, block_count, BC, feature_width)
    return split_grid.transpose(1, 0, 2, 3).reshape(block_count, row_count * BC, feature_width)


def from_blocks(blocks):
    block_count = blocks.shape[0]
    feature_width = blocks.shape[-1]
    split_blocks = blocks.reshape(block_count, BR, BC, feature_width)
    return split_blocks.transpose(1, 0, 2, 3).reshape(BR, block_count * BC, feature_width)


def by_heads(blocks):
    split_blocks = blocks.reshape(blocks.shape[:-1] + (HEADS, HSIZE))
    return jnp.moveaxis(split_blocks, -2, 0)


def join_heads(parts):
    moved = jnp.moveaxis(parts, 0, -2)
    return moved.reshape(moved.shape[:-2] + (HD,))


def windows(blocks, window_span):
    block_count = blocks.shape[0] - window_span + 1
    return jnp.concatenate(
        [blocks[offset : offset + block_count] for offset in range(window_span)], axis=1
    )


def fold_into(summed, gradients, offset_base, block_tokens):
    gradient_count = gradients.shape[0]
    window_span = gradients.shape[1] // block_tokens
    for offset in range(window_span):
        summed = summed.at[offset_base + offset : offset_base + offset + gradient_count].add(
            gradients[:, offset * block_tokens : (offset + 1) * block_tokens]
        )
    return summed


def attend(
    head_query_rows,
    windowed_key_rows,
    windowed_value_rows,
    head_output_gradient,
    cap_key,
    cap_value,
    permitted_mask,
    with_cap,
):
    score_scale = HSIZE ** (-0.5)
    window_scores = jnp.where(
        permitted_mask,
        inner_product("huf,hlf->hul", head_query_rows, windowed_key_rows) * score_scale,
        -jnp.inf,
    )
    row_top = window_scores.max(-1, keepdims=True)
    if with_cap:
        s_c = inner_product("bqe,ce->bqc", head_query_rows, cap_key) * score_scale
        row_top = jnp.maximum(row_top, s_c.max(-1, keepdims=True))
    e_w = jnp.exp(window_scores - row_top)
    row_total = e_w.sum(-1, keepdims=True)
    if with_cap:
        e_c = jnp.exp(s_c - row_top)
        row_total = row_total + e_c.sum(-1, keepdims=True)
    p_w = e_w / row_total
    window_probabilities = p_w.astype(jnp.bfloat16)
    attended_output = inner_product("ois,osg->oig", window_probabilities, windowed_value_rows)
    window_prob_gradient = inner_product("huf,hlf->hul", head_output_gradient, windowed_value_rows)
    row_dot = (p_w * window_prob_gradient).sum(-1, keepdims=True)
    if with_cap:
        p_c = e_c / row_total
        polar_probabilities = p_c.astype(jnp.bfloat16)
        attended_output = attended_output + inner_product(
            "nzd,dx->nzx", polar_probabilities, cap_value
        )
        dp_c = inner_product("bqe,ce->bqc", head_output_gradient, cap_value)
        row_dot = row_dot + (p_c * dp_c).sum(-1, keepdims=True)
    window_score_gradient = (p_w * (window_prob_gradient - row_dot)).astype(jnp.bfloat16)
    query_gradient_term = inner_product("ois,osg->oig", window_score_gradient, windowed_key_rows)
    key_gradient_terms = (
        inner_product("ydw,ydt->ywt", window_score_gradient, head_query_rows) * score_scale
    )
    value_gradient_terms = inner_product("ydw,ydt->ywt", window_probabilities, head_output_gradient)
    if with_cap:
        polar_score_gradient = (p_c * (dp_c - row_dot)).astype(jnp.bfloat16)
        query_gradient_term = query_gradient_term + inner_product(
            "nzd,dx->nzx", polar_score_gradient, cap_key
        )
        cap_key_terms = (
            inner_product("bqc,bqe->ce", polar_score_gradient, head_query_rows) * score_scale
        )
        cap_value_terms = inner_product("bqc,bqe->ce", polar_probabilities, head_output_gradient)
    else:
        cap_key_terms = jnp.zeros(cap_key.shape, jnp.float32)
        cap_value_terms = jnp.zeros(cap_value.shape, jnp.float32)
    query_gradient_term = query_gradient_term * score_scale
    log_total = row_top[..., 0] + jnp.log(row_total[..., 0])
    return (
        attended_output,
        query_gradient_term,
        key_gradient_terms,
        value_gradient_terms,
        cap_key_terms,
        cap_value_terms,
        log_total,
        row_dot[..., 0],
    )


def shards(query, keys, values, grad_out, band_width, cap_blocks):
    row_count = query.shape[0]
    col_count = query.shape[1]
    feature_width = query.shape[2]
    block_count = col_count // BC
    block_tokens = row_count * BC
    window_span = 2 * HALO + 1
    rim_cols = HALO * BC
    zero_index = jnp.zeros((), jnp.int32)
    lat_here = lax.axis_index("lat")
    lon_here = lax.axis_index("lon")
    is_pole = (lat_here == 0) | (lat_here == lax.axis_size("lat") - 1)
    band_reach = band_width[lat_here]
    key_value = jnp.stack([keys, values], 0)
    rimmed = padded(key_value, (("lon", 2),), rim_cols)
    first_row = jnp.where(lat_here == 0, 0, row_count - CR).astype(jnp.int32)
    cap_owner = cap_blocks[lon_here]
    cap_piece = lax.dynamic_slice(
        key_value, (zero_index, first_row, cap_owner * BC, zero_index), (2, CR, BC, feature_width)
    )
    cap_pair = lax.all_gather(
        cap_piece.reshape(2, CR * BC, feature_width), "lon", axis=1, tiled=True
    )
    windowed_key_rows = windows(to_blocks(rimmed[0], block_count + 2 * HALO), window_span)
    windowed_value_rows = windows(to_blocks(rimmed[1], block_count + 2 * HALO), window_span)
    offsets = jnp.arange(window_span * block_tokens, dtype=jnp.int32) // block_tokens
    permitted_mask = jnp.abs(offsets - HALO) <= band_reach
    head_inputs = (
        by_heads(to_blocks(query, block_count)),
        by_heads(windowed_key_rows),
        by_heads(windowed_value_rows),
        by_heads(to_blocks(grad_out, block_count)),
        by_heads(cap_pair[0]),
        by_heads(cap_pair[1]),
    )

    def make_branch(with_cap):

        def per_head(inputs_head):
            return attend(*inputs_head, permitted_mask, with_cap)

        def branch_body():
            return lax.map(per_head, head_inputs)

        return branch_body

    results = lax.cond(is_pole, make_branch(True), make_branch(False))
    out_h, dq_h, dkw_h, dvw_h, dkc_h, dvc_h, log_h, dot_h = results
    attended = from_blocks(join_heads(out_h)).astype(jnp.bfloat16)
    query_grad = from_blocks(join_heads(dq_h)).astype(jnp.bfloat16)
    empty_extended = jnp.zeros((block_count + 2 * HALO, block_tokens, feature_width), jnp.float32)
    extended_keys = fold_into(empty_extended, join_heads(dkw_h), 0, block_tokens)
    extended_values = fold_into(empty_extended, join_heads(dvw_h), 0, block_tokens)
    extended = jnp.stack([extended_keys, extended_values], 0)
    from_east = from_behind(extended[:, :HALO], "lon", -1)
    from_west = from_behind(extended[:, block_count + HALO :], "lon", 1)
    own_grads = extended[:, HALO : HALO + block_count]
    own_grads = own_grads.at[:, :HALO].add(from_west).at[:, block_count - HALO :].add(from_east)
    cap_term = jnp.concatenate([join_heads(dkc_h), join_heads(dvc_h)], axis=1)
    cap_back = lax.psum_scatter(cap_term, "lon", scatter_dimension=0, tiled=True)
    cap_back = cap_back.reshape(CR, BC, 2, feature_width).transpose(2, 0, 1, 3)
    grids = jnp.stack([from_blocks(own_grads[0]), from_blocks(own_grads[1])], 0)
    corner = (zero_index, first_row, cap_owner * BC, zero_index)
    current = lax.dynamic_slice(grids, corner, (2, CR, BC, feature_width))
    grids = lax.dynamic_update_slice(grids, current + cap_back, corner)
    return (attended, query_grad, grids[0].astype(jnp.bfloat16), grids[1].astype(jnp.bfloat16))


def solution(mesh):
    placed = (
        P(("dp", "lat"), "lon", None),
        P(("dp", "lat"), "lon", None),
        P(("dp", "lat"), "lon", None),
        P(("dp", "lat"), "lon", None),
        P(),
        P(),
    )
    return jax.shard_map(
        shards,
        mesh=mesh,
        in_specs=placed,
        out_specs=(
            P(("dp", "lat"), "lon", None),
            P(("dp", "lat"), "lon", None),
            P(("dp", "lat"), "lon", None),
            P(("dp", "lat"), "lon", None),
        ),
        check_vma=False,
    )
```

profile of v0, /device:TPU:1, one launch (start us, length us, event | category | flops | bytes accessed | tf_op | source)
XLA Modules:
  0.0 280.9 jit_solution(1398238909883036505)
XLA Ops:
  7.2 2.3 fusion.155
  9.5 2.6 collective-permute-start
  16.6 22.7 %all-gather = bf16[2,1,256,512]{3,2,1,0:T(8,128)(2,1)S(1)} all-gather(bf16[2,1,16,512]{3,2,1,0:T(8,128)(2,1)S(1)} %fusion.159), channel_id=2, replica_groups=mesh['lon'=16,'lat'=8,'dp'=2] {'lon'}, dimensions={2}, use_global_device_ids=true | all-gather | bytes 557056 | tf_op jit(solution)/shard_map/all_gather | solution.py:169
  45.1 1.5 concatenate.63
  46.7 2.3 concatenate.62
  49.0 2.3 concatenate.61
  51.3 2.3 concatenate.60
  53.6 2.3 concatenate.59
  57.2 1.5 concatenate.69
  58.7 2.3 concatenate.68
  61.1 2.3 concatenate.67
  63.3 2.4 concatenate.66
  67.0 2.3 constant_dynamic-update-slice_fusion.9
  78.6 120.7 %conditional.1 = (bf16[8,3,128,64]{2,3,1,0:T(8,128)(2,1)}, bf16[8,3,128,64]{2,3,1,0:T(8,128)(2,1)}, f32[8,3,640,64]{2,3,1,0:T(8,128)}, f32[8,3,640,64]{2,3,1,0:T...) conditional(s32[]{:T(128)} %convert_element_type.61, (pred[640]{0:T(1024)(128)(4,1)S(1)}, ...), branch_computations={%region_0.6_spmd, %region_6.15_spmd} | conditional | flops 271235968 | bytes 27366248 | solution.py:195
  79.7 5.8 %copy.52 = bf16[8,3,640,64]{2,3,1,0:T(8,128)(2,1)} copy(bf16[8,3,640,64]{3,0,2,1:T(8,128)(2,1)} %get-tuple-element.401) | data formatting | bytes 3932160 | tf_op jit(solution)/shard_map
  85.4 4.7 %copy.51 = bf16[8,3,640,64]{2,3,1,0:T(8,128)(2,1)S(1)} copy(bf16[8,3,640,64]{3,0,2,1:T(8,128)(2,1)} %get-tuple-element.399) | data formatting | bytes 3932160 | tf_op jit(solution)/shard_map
  90.2 108.3 %while.51 = (s32[]{:T(128)}, bf16[8,3,128,64]{2,3,1,0:T(8,128)(2,1)S(1)}, bf16[8,3,128,64]{2,3,1,0:T(8,128)(2,1)}, f32[8,3,640,64]{2,3,1,0:T(8,128)}, f32[8,3,64...) while((s32[]{:T(128)}, ...), condition=%wide.region_14.14_spmd, body=%wide.region_7.13_spmd.sunk | while | flops 271235968 | bytes 16355997 | solution.py:191
  92.3 1.4 fusion.251
  96.9 1.4 multiply_reduce_fusion.6
  99.2 1.6 fusion.254
  105.9 1.4 fusion.251
  112.7 1.6 fusion.254
  119.4 1.4 fusion.251
  124.0 1.4 multiply_reduce_fusion.6
  126.3 1.6 fusion.254
  133.0 1.4 fusion.251
  137.6 1.4 multiply_reduce_fusion.6
  139.8 1.6 fusion.254
  146.5 1.4 fusion.251
  153.4 1.6 fusion.254
  160.0 1.4 fusion.251
  164.6 1.4 multiply_reduce_fusion.6
  166.9 1.6 fusion.254
  173.6 1.4 fusion.251
  178.1 1.4 multiply_reduce_fusion.6
  180.4 1.6 fusion.254
  187.1 1.4 fusion.251
  191.7 1.4 multiply_reduce_fusion.6
  194.0 1.6 fusion.254
  199.2 2.4 copy.58
  202.5 1.8 copy-done.2
  212.5 7.1 %collective-permute-done.2 = f32[2,2,128,512]{2,3,1,0:T(8,128)} collective-permute-done((f32[2,2,128,512]{2,3,1,0:T(8,128)}, f32[2,2,128,512]{2,3,1,0:T(8,128)}, u32[]{:S(2)}, u32[]{:S(2)}) %collective-permute-start.2) | collective-permute-done | bytes 1048608 | tf_op jit(solution)/shard_map/ppermute | solution.py:31
  219.6 2.4 pad_maximum_fusion.2
  221.9 4.6 %collective-permute-start.3 = (f32[2,2,128,512]{2,3,1,0:T(8,128)}, f32[2,2,128,512]{2,3,1,0:T(8,128)}, u32[]{:S(2)}, u32[]{:S(2)}) collective-permute-start(f32[2,2,128,512]{2,3,1,0:T(8,128)} %get-tuple-element.466), channel_id=1, source_target_pairs={{0,240},{16,0},{32,16},{48,32},{64,48},{80,64},{96,80},{112,96},{1... | collective-permute-start | bytes 3145736 | tf_op jit(solution)/shard_map/ppermute | solution.py:31
  226.6 1.4 copy.56
  230.9 7.7 %collective-permute-done.3 = f32[2,2,128,512]{2,3,1,0:T(8,128)} collective-permute-done((f32[2,2,128,512]{2,3,1,0:T(8,128)}, f32[2,2,128,512]{2,3,1,0:T(8,128)}, u32[]{:S(2)}, u32[]{:S(2)}) %collective-permute-start.3) | collective-permute-done | bytes 1048608 | tf_op jit(solution)/shard_map/ppermute | solution.py:31
  238.6 1.4 fusion.144
  242.6 29.5 %reduce-scatter.2.cloned.1.call-done = f32[16,1024]{1,0:T(8,128)} async-done(((f32[256,1024]{1,0:T(8,128)}), f32[16,1024]{1,0:T(8,128)}) %reduce-scatter.2.cloned.1.call-update) | async-done | bytes 65552 | tf_op jit(solution)/shard_map/reduce_scatter | solution.py:208
  (239 shorter events, 115.2 us)
Async XLA Ops:
  7.2 7.5 %copy-start.14 = (bf16[8,48,512]{2,1,0:T(8,128)(2,1)S(1)}, bf16[8,48,512]{2,1,0:T(8,128)(2,1)}, u32[]{:S(2)}) copy-start(bf16[8,48,512]{2,1,0:T(8,128)(2,1)} %param.36) | copy-start | bytes 1179652
  7.2 265.0 %reduce-scatter.2.cloned.1.call-start = ((), (), s32[]{:S(2)}) async-start(), calls=%async_computation.1 | async-start | bytes 1114112 | tf_op jit(solution)/shard_map/reduce_scatter | solution.py:208
  9.5 32.8 %collective-permute-start = (bf16[2,8,32,512]{3,2,1,0:T(8,128)(2,1)}, bf16[2,8,32,512]{3,2,1,0:T(8,128)(2,1)S(1)}, u32[]{:S(2)}, u32[]{:S(2)}) collective-permute-start(bf16[2,8,32,512]{3,2,1,0:T(8,128)(2,1)} %get-tuple-element.484), channel_id=1, source_target_pairs={{0,16},{16,32},{32,48},{48,64},{64,80},{80,96},{96,112},{112,128},... | collective-permute-start | bytes 1572872 | tf_op jit(solution)/shard_map/ppermute | solution.py:22
  12.1 30.2 %collective-permute-start.1 = (bf16[2,8,32,512]{3,2,1,0:T(8,128)(2,1)}, bf16[2,8,32,512]{3,2,1,0:T(8,128)(2,1)}, u32[]{:S(2)}, u32[]{:S(2)}) collective-permute-start(bf16[2,8,32,512]{3,2,1,0:T(8,128)(2,1)} %get-tuple-element.485), channel_id=1, source_target_pairs={{16,0},{32,16},{48,32},{64,48},{80,64},{96,80},{112,96},{128,112},... | collective-permute-start | bytes 1572872 | tf_op jit(solution)/shard_map/ppermute | solution.py:23
  14.7 1.9 copy-start.3
  14.7 1.9 copy-start.4
  16.5 24.5 %copy-start.17 = (s32[8]{0:T(128)S(1)}, s32[8]{0:T(128)}, u32[]{:S(2)}) copy-start(s32[8]{0:T(128)} %param.40) | copy-start | bytes 100
  58.7 7.0 %copy-start.13 = (bf16[3,8,16,512]{3,2,1,0:T(8,128)(2,1)S(1)}, bf16[3,8,16,512]{3,2,1,0:T(8,128)(2,1)}, u32[]{:S(2)}) copy-start(bf16[3,8,16,512]{3,2,1,0:T(8,128)(2,1)} %get-tuple-element.476) | copy-start | bytes 1179652
  67.0 2.3 copy-start.8
  67.0 3.3 %copy-start.11 = (bf16[3,128,8,64]{3,2,1,0:T(8,128)(2,1)S(1)}, bf16[3,128,8,64]{3,2,1,0:T(8,128)(2,1)}, u32[]{:S(2)}) copy-start(bf16[3,128,8,64]{3,2,1,0:T(8,128)(2,1)} %concatenate.66) | copy-start | bytes 1179652
  69.3 2.0 copy-start.10
  70.3 2.1 copy-start.9
  72.4 2.0 copy-start.7
  73.4 2.1 copy-start.6
  74.4 2.1 copy-start.5
  198.5 0.7 copy-start.15
  202.2 2.1 copy-start.2
  205.8 1.6 copy-start
  207.4 12.2 %collective-permute-start.2 = (f32[2,2,128,512]{2,3,1,0:T(8,128)}, f32[2,2,128,512]{2,3,1,0:T(8,128)}, u32[]{:S(2)}, u32[]{:S(2)}) collective-permute-start(f32[2,2,128,512]{2,3,1,0:T(8,128)} %fusion.140), channel_id=1, source_target_pairs={{0,16},{16,32},{32,48},{48,64},{64,80},{80,96},{96,112},{112,128},... | collective-permute-start | bytes 3145736 | tf_op jit(solution)/shard_map/ppermute | solution.py:31
  211.1 8.5 %copy-start.1 = (f32[1,7,128,512]{2,3,1,0:T(8,128)S(1)}, f32[1,7,128,512]{2,3,1,0:T(8,128)}, u32[]{:S(2)}) copy-start(f32[1,7,128,512]{2,3,1,0:T(8,128)} %copy-done) | copy-start | bytes 5505028
  221.9 7.3 %copy-start.16 = (bf16[8,3,128,64]{2,3,1,0:T(8,128)(2,1)S(1)}, bf16[8,3,128,64]{2,3,1,0:T(8,128)(2,1)}, u32[]{:S(2)}) copy-start(bf16[8,3,128,64]{2,3,1,0:T(8,128)(2,1)} %get-tuple-element.356) | copy-start | bytes 1179652
  221.9 16.7 %collective-permute-start.3 = (f32[2,2,128,512]{2,3,1,0:T(8,128)}, f32[2,2,128,512]{2,3,1,0:T(8,128)}, u32[]{:S(2)}, u32[]{:S(2)}) collective-permute-start(f32[2,2,128,512]{2,3,1,0:T(8,128)} %get-tuple-element.466), channel_id=1, source_target_pairs={{0,240},{16,0},{32,16},{48,32},{64,48},{80,64},{96,80},{112,96},{1... | collective-permute-start | bytes 3145736 | tf_op jit(solution)/shard_map/ppermute | solution.py:31
  241.1 1.1 copy-start.12
Sparse Core Ops, SparseCore 0:
  211.2 60.9 reduce-scatter.1
where the time goes:
time: 286 us; the launch traced here: 281 us
  matrix products  99.1 us (35%)
  local copies, waits for them, and re-layouts  69.4 us (24%)
  waiting for transfers between devices  44.4 us (16%)
  blocking collectives  22.7 us (8%)
  other arithmetic  21.9 us (8%)
  between operations  15.1 us (5%)
  starting transfers between devices  8.03 us (3%)
    dot_general x96, matrix products, inner_product(): jnp.einsum(form, left_side, right_side, preferred_element_type=jnp.float32)  99.1 us
    reduce_scatter x1, waiting for transfers between devices, shards(): lax.psum_scatter(cap_term, 'lon', scatter_dimension=0, tiled=True)  29.5 us
    all_gather x1, blocking collectives, shards(): lax.all_gather(cap_piece.reshape(2, CR * BC, feature_width), 'lon', axis=...  22.7 us
    concatenate x12, local copies, waits for them, and re-layouts, windows(): jnp.concatenate([blocks[offset:offset + block_count] for offset in range(...  22.6 us
    ppermute x2, waiting for transfers between devices, from_behind(): return lax.ppermute(value, axis, pairs)  14.8 us
    unnamed x44, local copies, waits for them, and re-layouts  12.8 us
    another operation x4, local copies, waits for them, and re-layouts  11.6 us
  transfers between devices with their start and end apart: 5, of which 3 were waited for; matrix products, arithmetic and copies ran while one was open for 7% of the time, Pallas kernels for 0%

commit v1 on v0

v1 whole, which is shorter than its diff:
```python
import functools

import jax
import jax.numpy as jnp
from jax import lax
from jax.experimental import pallas as pl
from jax.experimental.pallas import tpu as pltpu
from jax.sharding import PartitionSpec as P

HEADS = 8
HSIZE = 64
BR = 8
BC = 16
NB = 3
HALO = 2
CR = 1
BANDS = 8
HD = 512
PAIR = 2 * HSIZE
PAIRS = HD // PAIR
TOK = BR * BC
LON = 16
SPAN = 2 * HALO + 1
EXT = NB + 2 * HALO
CAPK = LON * CR * BC
CAP0 = EXT * TOK
KEYS = CAP0 + CAPK
RIM = HALO * BC
FAR = -1e30
STEPS = (8, 4, 2, 1)
VMEM = 56 * 1024 * 1024
F32 = jnp.float32
BF16 = jnp.bfloat16


def swap(value, mask):
    return lax.ppermute(value, "lon", [(i, i ^ mask) for i in range(LON)])


def shift(value, steps):
    return lax.ppermute(value, "lon", [(i, (i + steps) % LON) for i in range(LON)])


def params():
    return pltpu.CompilerParams(vmem_limit_bytes=VMEM)


def vmem(count):
    return [pl.BlockSpec(memory_space=pltpu.VMEM)] * count


def smem():
    return pl.BlockSpec(memory_space=pltpu.SMEM)


def nt(left, right):
    return lax.dot_general(left, right, (((1,), (1,)), ((), ())), preferred_element_type=F32)


def nn(left, right):
    return lax.dot_general(left, right, (((1,), (0,)), ((), ())), preferred_element_type=F32)


def pole_row(here_ref):
    return jnp.where(here_ref[0] == 0, 0, BR - CR)


def cap_column(here_ref, cap_blocks_ref):
    return pl.multiple_of(cap_blocks_ref[here_ref[1]] * BC, BC)


def edges_kernel(here_ref, cap_blocks_ref, k_ref, v_ref, east_ref, west_ref, cap_ref):
    row = pole_row(here_ref)
    column = cap_column(here_ref, cap_blocks_ref)
    for n, ref in enumerate((k_ref, v_ref)):
        cap_ref[0, n] = ref[row, pl.ds(column, BC), :]
        east_ref[n] = ref[:, NB * BC - RIM :, :]
        west_ref[n] = ref[:, :RIM, :]


def edges(here, cap_blocks, keys, values):
    rim = jax.ShapeDtypeStruct((2, BR, RIM, HD), BF16)
    return pl.pallas_call(
        edges_kernel,
        out_shape=(rim, rim, jax.ShapeDtypeStruct((1, 2, BC, HD), BF16)),
        in_specs=[smem(), smem()] + vmem(2),
        out_specs=tuple(vmem(3)),
        compiler_params=params(),
    )(here, cap_blocks, keys, values)


def block_of(ref, prefix, column, lanes):
    block = ref[prefix + (slice(None), pl.ds(column, BC), lanes)]
    return block.reshape(TOK, PAIR)


def masked_heads(block):
    lane = lax.broadcasted_iota(jnp.int32, block.shape, 1)
    zero = jnp.zeros_like(block)
    return jnp.concatenate(
        [jnp.where(lane < HSIZE, block, zero), jnp.where(lane < HSIZE, zero, block)], axis=0
    )


def attend_kernel(
    here_ref,
    width_ref,
    q_ref,
    k_ref,
    v_ref,
    d_ref,
    west_ref,
    east_ref,
    cap_ref,
    o_ref,
    dq_ref,
    own_ref,
    to_west_ref,
    to_east_ref,
    cap_keep_ref,
    cap_send_ref,
    kx,
    vx,
    kt,
    vt,
    dk,
    dv,
):
    lat = here_ref[0]
    width = width_ref[lat]
    pole = (lat == 0) | (lat == BANDS - 1)
    window_bias = [
        jnp.where(abs(offset - HALO) <= width, 0.0, FAR).astype(F32) for offset in range(SPAN)
    ]
    cap_bias = jnp.where(pole, 0.0, FAR).astype(F32)
    biases = window_bias + [cap_bias] * (CAPK // TOK)
    scale = HSIZE**-0.5

    def pair_body(pair, carry):
        lanes = pl.ds(pl.multiple_of(pair * PAIR, PAIR), PAIR)
        for n, (ref, flat, turned) in enumerate(((k_ref, kx, kt), (v_ref, vx, vt))):
            for j in range(EXT + CAPK // TOK):
                if j < HALO:
                    block = block_of(west_ref, (n,), j * BC, lanes)
                elif j < HALO + NB:
                    block = block_of(ref, (), (j - HALO) * BC, lanes)
                elif j < EXT:
                    block = block_of(east_ref, (n,), (j - HALO - NB) * BC, lanes)
                else:
                    first = (j - EXT) * (TOK // BC)
                    block = cap_ref[first : first + TOK // BC, n, :, lanes].reshape(TOK, PAIR)
                flat[j * TOK : (j + 1) * TOK, :] = block
                turned[:, j * TOK : (j + 1) * TOK] = block.T
        dk[...] = jnp.zeros_like(dk)
        dv[...] = jnp.zeros_like(dv)
        for i in range(NB):
            window = pl.ds(i * TOK, SPAN * TOK)
            cap = pl.ds(CAP0, CAPK)
            query = masked_heads(block_of(q_ref, (), i * BC, lanes) * jnp.asarray(scale, BF16))
            grad = masked_heads(block_of(d_ref, (), i * BC, lanes))
            scores = [nt(kx[part, :], query) for part in (window, cap)]
            scores = [
                part[n * TOK : (n + 1) * TOK]
                for part in scores
                for n in range(part.shape[0] // TOK)
            ]
            top = functools.reduce(
                jnp.maximum,
                [s.max(0, keepdims=True) + b for s, b in zip(scores, biases)],
            )
            weights = [jnp.exp(s - (top - b)) for s, b in zip(scores, biases)]
            total = functools.reduce(jnp.add, [w.sum(0, keepdims=True) for w in weights])
            inverse = 1.0 / total
            weights = [w * inverse for w in weights]
            grads = [nt(vx[part, :], grad) for part in (window, cap)]
            grads = [
                part[n * TOK : (n + 1) * TOK] for part in grads for n in range(part.shape[0] // TOK)
            ]
            dot = functools.reduce(
                jnp.add, [(w * g).sum(0, keepdims=True) for w, g in zip(weights, grads)]
            )
            slopes = [(w * (g - dot)).astype(BF16) for w, g in zip(weights, grads)]
            weights = [w.astype(BF16) for w in weights]
            parts = ((window, 0, SPAN), (cap, SPAN, len(weights)))
            out = jnp.zeros((PAIR, 2 * TOK), F32)
            turn = jnp.zeros((PAIR, 2 * TOK), F32)
            for part, low, high in parts:
                weight = jnp.concatenate(weights[low:high], axis=0)
                slope = jnp.concatenate(slopes[low:high], axis=0)
                out += nn(vt[:, part], weight)
                turn += nn(kt[:, part], slope)
                dv[part, :] += nn(weight, grad)
                dk[part, :] += nn(slope, query)
            for ref, value in ((o_ref, out), (dq_ref, turn * scale)):
                value = jnp.concatenate([value[:HSIZE, :TOK], value[HSIZE:, TOK:]], axis=0)
                ref[:, i * BC : (i + 1) * BC, lanes] = value.T.astype(BF16).reshape(BR, BC, PAIR)
        for n, grads in enumerate((dk, dv)):
            for j in range(EXT):
                block = grads[j * TOK : (j + 1) * TOK, :].reshape(BR, BC, PAIR)
                if j < HALO:
                    to_west_ref[n, :, j * BC : (j + 1) * BC, lanes] = block.astype(BF16)
                elif j < HALO + NB:
                    own_ref[n, :, (j - HALO) * BC : (j - HALO + 1) * BC, lanes] = block
                else:
                    column = (j - HALO - NB) * BC
                    to_east_ref[n, :, column : column + BC, lanes] = block.astype(BF16)
            half = CAPK // 2
            cap_keep_ref[:, n, :, lanes] = grads[CAP0 : CAP0 + half, :].reshape(LON // 2, BC, PAIR)
            cap_send_ref[:, n, :, lanes] = (
                grads[CAP0 + half :, :].reshape(LON // 2, BC, PAIR).astype(BF16)
            )
        return carry

    lax.fori_loop(0, PAIRS, pair_body, 0)


def attend(here, band_width, query, keys, values, grad_out, west, east, cap):
    rim = jax.ShapeDtypeStruct((2, BR, RIM, HD), BF16)
    grid = jax.ShapeDtypeStruct(query.shape, BF16)
    return pl.pallas_call(
        attend_kernel,
        out_shape=(
            grid,
            grid,
            jax.ShapeDtypeStruct((2,) + query.shape, F32),
            rim,
            rim,
            jax.ShapeDtypeStruct((LON // 2, 2, BC, HD), F32),
            jax.ShapeDtypeStruct((LON // 2, 2, BC, HD), BF16),
        ),
        in_specs=[smem(), smem()] + vmem(7),
        out_specs=tuple(vmem(7)),
        scratch_shapes=[
            pltpu.VMEM((KEYS, PAIR), BF16),
            pltpu.VMEM((KEYS, PAIR), BF16),
            pltpu.VMEM((PAIR, KEYS), BF16),
            pltpu.VMEM((PAIR, KEYS), BF16),
            pltpu.VMEM((KEYS, PAIR), F32),
            pltpu.VMEM((KEYS, PAIR), F32),
        ],
        compiler_params=params(),
    )(here, band_width, query, keys, values, grad_out, west, east, cap)


def join_kernel(
    here_ref, cap_blocks_ref, own_ref, west_ref, east_ref, keep_ref, cap_ref, dk_ref, dv_ref, total
):
    row = pole_row(here_ref)
    column = cap_column(here_ref, cap_blocks_ref)
    for n, ref in enumerate((dk_ref, dv_ref)):
        total[...] = own_ref[n]
        total[:, :RIM, :] += west_ref[n].astype(F32)
        total[:, NB * BC - RIM :, :] += east_ref[n].astype(F32)
        total[row, pl.ds(column, BC), :] += keep_ref[0, n] + cap_ref[0, n].astype(F32)
        ref[...] = total[...].astype(BF16)


def join(here, cap_blocks, own, west, east, keep, cap):
    grid = jax.ShapeDtypeStruct(own.shape[1:], BF16)
    return pl.pallas_call(
        join_kernel,
        out_shape=(grid, grid),
        in_specs=[smem(), smem()] + vmem(5),
        out_specs=tuple(vmem(2)),
        scratch_shapes=[pltpu.VMEM(own.shape[1:], F32)],
        compiler_params=params(),
    )(here, cap_blocks, own, west, east, keep, cap)


def shards(query, keys, values, grad_out, band_width, cap_blocks):
    here = jnp.stack([lax.axis_index("lat"), lax.axis_index("lon")]).astype(jnp.int32)
    to_east, to_west, cap = edges(here, cap_blocks, keys, values)
    west = shift(to_east, 1)
    east = shift(to_west, -1)
    for mask in STEPS:
        cap = jnp.concatenate([cap, swap(cap, mask)], axis=0)
    attended, query_grad, own, to_west, to_east, keep, send = attend(
        here, band_width, query, keys, values, grad_out, west, east, cap
    )
    east = shift(to_west, -1)
    west = shift(to_east, 1)
    for mask in STEPS[:0:-1]:
        total = keep + swap(send, mask).astype(F32)
        half = total.shape[0] // 2
        keep, send = total[:half], total[half:].astype(BF16)
    cap = swap(send, STEPS[0])
    key_grad, value_grad = join(here, cap_blocks, own, west, east, keep, cap)
    return attended, query_grad, key_grad, value_grad


def solution(mesh):
    grid = P(("dp", "lat"), "lon", None)
    return jax.shard_map(
        shards,
        mesh=mesh,
        in_specs=(grid, grid, grid, grid, P(), P()),
        out_specs=(grid, grid, grid, grid),
        check_vma=False,
    )
```

time: 286 us -> 72 us (0.25); the launches traced: 281 us -> 71.5 us
  matrix products: 99.1 us -> 0 us
  local copies, waits for them, and re-layouts: 69.4 us -> 3.25 us
  waiting for transfers between devices: 44.4 us -> 20.5 us
  blocking collectives: 22.7 us -> 0 us
  Pallas kernels: 0 us -> 21.5 us
  other arithmetic: 21.9 us -> 4.1 us
  between operations: 15.1 us -> 0.76 us
  starting transfers between devices: 8.03 us -> 21.4 us
    dot_general x96 -> x0, matrix products: 99.1 us -> none  [inner_product(): jnp.einsum(form, left_side, right_side, preferred_element_type=jnp.float32)]
    reduce_scatter x1 -> x0, waiting for transfers between devices: 29.5 us -> none  [shards(): lax.psum_scatter(cap_term, 'lon', scatter_dimension=0, tiled=True)]
    all_gather x1 -> x0, blocking collectives: 22.7 us -> none  [shards(): lax.all_gather(cap_piece.reshape(2, CR * BC, feature_width), 'lon', axis=...]
    concatenate x12 -> x1, local copies, waits for them, and re-layouts: 22.6 us -> 0.02 us  [shards(): cap = jnp.concatenate([cap, swap(cap, mask)], axis=0)]
    pallas_call x0 -> x3, Pallas kernels: none -> 21.5 us  [the longest x1 16.6 us: attend(): pl.pallas_call(attend_kernel, out_shape=(grid, grid, jax.ShapeDtypeStruct...]
    ppermute x4 -> x12, starting transfers between devices: 7.99 us -> 21.4 us  [the longest x8 14.2 us: swap(): return lax.ppermute(value, 'lon', [(i, i ^ mask) for i in range(LON)])]
    another operation x8 -> x0, local copies, waits for them, and re-layouts: 12.5 us -> none
    unnamed x44 -> x20, local copies, waits for them, and re-layouts: 12.8 us -> 2.56 us
  transfers between devices with their start and end apart: 5 -> 12, of which waited for: 3 -> 9; matrix products, arithmetic and copies ran while one was open for 7% -> 3% of each run, Pallas kernels for 0% -> 0%
where the time goes in v1:
time: 72 us; the launch traced here: 71.5 us
  Pallas kernels  21.5 us (30%)
  starting transfers between devices  21.4 us (30%)
  waiting for transfers between devices  20.5 us (28%)
  other arithmetic  4.1 us (6%)
  local copies, waits for them, and re-layouts  3.25 us (5%)
  between operations  0.76 us (1%)
    ppermute x8, waiting for transfers between devices, swap(): return lax.ppermute(value, 'lon', [(i, i ^ mask) for i in range(LON)])  16.9 us
    pallas_call x1, Pallas kernels, attend(): pl.pallas_call(attend_kernel, out_shape=(grid, grid, jax.ShapeDtypeStruct...  16.6 us
    ppermute x8, starting transfers between devices, swap(): return lax.ppermute(value, 'lon', [(i, i ^ mask) for i in range(LON)])  14.2 us
    ppermute x4, starting transfers between devices, shift(): lax.ppermute(value, 'lon', [(i, (i + steps) % LON) for i in range(LON)])  7.12 us
    ppermute x4, waiting for transfers between devices, shift(): lax.ppermute(value, 'lon', [(i, (i + steps) % LON) for i in range(LON)])  3.59 us
    pallas_call x1, Pallas kernels, join(): pl.pallas_call(join_kernel, out_shape=(grid, grid), in_specs=[smem(), sme...  2.78 us
    unnamed x20, local copies, waits for them, and re-layouts  2.56 us
    concatenate x3, other arithmetic, shards(): cap = jnp.concatenate([cap, swap(cap, mask)], axis=0)  2.32 us
  transfers between devices with their start and end apart: 12, of which 9 were waited for; matrix products, arithmetic and copies ran while one was open for 3% of the time, Pallas kernels for 0%

profile of v1, /device:TPU:1, one launch (start us, length us, event | category | flops | bytes accessed | tf_op | source)
XLA Modules:
  0.0 71.5 jit_solution(4367251543516139737)
XLA Ops:
  0.6 0.6 pad_add_fusion.here_ref
  1.2 2.2 %shard_map.93 = (bf16[2,8,32,512]{3,2,1,0:T(8,128)(2,1)}, bf16[2,8,32,512]{3,2,1,0:T(8,128)(2,1)}, bf16[1,2,16,512]{3,2,1,0:T(8,128)(2,1)}) custom-call(s32[2]{0:T(128)} %pad_add_fusion.here_ref, s32[16]{0:T(128)} %cap_blocks_ref.3, bf16[8,48,512]{2,1,0:T(8,128)(2,1)} %k_ref.3, bf16[8,48,512]{2,1,0:T(8,128)(2,1)} %v_ref.3), custom_call_target="tpu_custom_call" | custom-call | tf_op jit(solution)/shard_map/pallas_call | solution.py:83
  3.4 2.1 %collective-permute-start.2 = (bf16[1,2,16,512]{3,2,1,0:T(8,128)(2,1)}, bf16[1,2,16,512]{3,2,1,0:T(8,128)(2,1)S(1)}, u32[]{:S(2)}, u32[]{:S(2)}) collective-permute-start(bf16[1,2,16,512]{3,2,1,0:T(8,128)(2,1)} %get-tuple-element.18), channel_id=1, source_target_pairs={{0,128},{16,144},{32,160},{48,176},{64,192},{80,208},{96,224},{112... | collective-permute-start | bytes 98312 | tf_op jit(solution)/shard_map/ppermute | solution.py:37
  5.5 1.5 %collective-permute-done.2 = bf16[1,2,16,512]{3,2,1,0:T(8,128)(2,1)S(1)} collective-permute-done((bf16[1,2,16,512]{3,2,1,0:T(8,128)(2,1)}, bf16[1,2,16,512]{3,2,1,0:T(8,128)(2,1)S(1)}, u32[]{:S(2)}, u32[]{:S(2)}) %collective-permute-start.2) | collective-permute-done | bytes 32800 | tf_op jit(solution)/shard_map/ppermute | solution.py:37
  7.0 0.8 %pad_maximum_fusion.2 = bf16[2,2,16,512]{3,2,1,0:T(8,128)(2,1)S(1)} fusion(bf16[1,2,16,512]{3,2,1,0:T(8,128)(2,1)S(1)} %collective-permute-done.2, bf16[1,2,16,512]{3,2,1,0:T(8,128)(2,1)} %get-tuple-element.18), kind=kLoop, calls=%fused_computation.8 | loop fusion | flops 32768 | bytes 131072 | tf_op jit(solution)/shard_map/concatenate | solution.py:276
  7.8 2.9 %collective-permute-start.3 = (bf16[2,2,16,512]{3,2,1,0:T(8,128)(2,1)S(1)}, bf16[2,2,16,512]{3,2,1,0:T(8,128)(2,1)S(1)}, u32[]{:S(2)}, u32[]{:S(2)}) collective-permute-start(bf16[2,2,16,512]{3,2,1,0:T(8,128)(2,1)S(1)} %pad_maximum_fusion.2), channel_id=1, source_target_pairs={{0,64},{16,80},{32,96},{48,112},{64,0},{80,16},{96,32},{112,48},{1... | collective-permute-start | bytes 196616 | tf_op jit(solution)/shard_map/ppermute | solution.py:37
  10.7 1.7 %collective-permute-done.3 = bf16[2,2,16,512]{3,2,1,0:T(8,128)(2,1)S(1)} collective-permute-done((bf16[2,2,16,512]{3,2,1,0:T(8,128)(2,1)S(1)}, bf16[2,2,16,512]{3,2,1,0:T(8,128)(2,1)S(1)}, u32[]{:S(2)}, u32[]{:S(2)}) %collective-permute-start.3) | collective-permute-done | bytes 65568 | tf_op jit(solution)/shard_map/ppermute | solution.py:37
  12.4 0.8 %pad_maximum_fusion.1 = bf16[4,2,16,512]{3,2,1,0:T(8,128)(2,1)S(1)} fusion(bf16[2,2,16,512]{3,2,1,0:T(8,128)(2,1)S(1)} %collective-permute-done.3, bf16[1,2,16,512]{3,2,1,0:T(8,128)(2,1)S(1)} %collective-permute-done.2, bf16[1,2,16,512]{3,2,1,0:T(8,128)(2,1)} %get-tuple-element.18), kind=kLoop, calls=%fused_computation.6 | loop fusion | flops 131072 | bytes 262144 | tf_op jit(solution)/shard_map/concatenate | solution.py:276
  13.2 1.5 %collective-permute-start.4 = (bf16[4,2,16,512]{3,2,1,0:T(8,128)(2,1)S(1)}, bf16[4,2,16,512]{3,2,1,0:T(8,128)(2,1)S(1)}, u32[]{:S(2)}, u32[]{:S(2)}) collective-permute-start(bf16[4,2,16,512]{3,2,1,0:T(8,128)(2,1)S(1)} %pad_maximum_fusion.1), channel_id=1, source_target_pairs={{0,32},{16,48},{32,0},{48,16},{64,96},{80,112},{96,64},{112,80},{1... | collective-permute-start | bytes 393224 | tf_op jit(solution)/shard_map/ppermute | solution.py:37
  14.7 5.1 %collective-permute-start = (bf16[2,8,32,512]{3,2,1,0:T(8,128)(2,1)}, bf16[2,8,32,512]{3,2,1,0:T(8,128)(2,1)S(1)}, u32[]{:S(2)}, u32[]{:S(2)}) collective-permute-start(bf16[2,8,32,512]{3,2,1,0:T(8,128)(2,1)} %get-tuple-element.16), channel_id=1, source_target_pairs={{0,16},{16,32},{32,48},{48,64},{64,80},{80,96},{96,112},{112,128},... | collective-permute-start | bytes 1572872 | tf_op jit(solution)/shard_map/ppermute | solution.py:41
  19.8 0.0 collective-permute-start.1
  19.8 0.8 %constant_dynamic-update-slice_fusion.4 = bf16[16,2,16,512]{3,2,1,0:T(8,128)(2,1)S(1)} fusion(bf16[1,2,16,512]{3,2,1,0:T(8,128)(2,1)} %get-tuple-element.18), kind=kLoop, calls=%fused_computation.13 | loop fusion | bytes 65536
  20.6 0.0 collective-permute-done.4
  20.6 0.8 %pad_maximum_fusion = bf16[8,2,16,512]{3,2,1,0:T(8,128)(2,1)S(1)} fusion(bf16[4,2,16,512]{3,2,1,0:T(8,128)(2,1)S(1)} %collective-permute-done.4, bf16[2,2,16,512]{3,2,1,0:T(8,128)(2,1)S(1)} %collective-permute-done.3, bf16[1,2,16,512]{3,2,1,0:T(8,128)(2,1)S(1)} %collective-permute-done.2, bf16[1,2,16,512]{3,2,1,0:T(8,128)(2,1)} %get-tuple-element.18), kind=kLoop, calls=%fused_computation.3 | loop fusion | flops 393216 | bytes 524288 | tf_op jit(solution)/shard_map/concatenate | solution.py:276
  21.4 2.7 %collective-permute-start.5 = (bf16[8,2,16,512]{3,2,1,0:T(8,128)(2,1)S(1)}, bf16[8,2,16,512]{3,2,1,0:T(8,128)(2,1)S(1)}, u32[]{:S(2)}, u32[]{:S(2)}) collective-permute-start(bf16[8,2,16,512]{3,2,1,0:T(8,128)(2,1)S(1)} %pad_maximum_fusion), channel_id=1, source_target_pairs={{0,16},{16,0},{32,48},{48,32},{64,80},{80,64},{96,112},{112,96},{1... | collective-permute-start | bytes 786440 | tf_op jit(solution)/shard_map/ppermute | solution.py:37
  24.0 1.1 %collective-permute-done.5 = bf16[8,2,16,512]{3,2,1,0:T(8,128)(2,1)S(1)} collective-permute-done((bf16[8,2,16,512]{3,2,1,0:T(8,128)(2,1)S(1)}, bf16[8,2,16,512]{3,2,1,0:T(8,128)(2,1)S(1)}, u32[]{:S(2)}, u32[]{:S(2)}) %collective-permute-start.5) | collective-permute-done | bytes 262176 | tf_op jit(solution)/shard_map/ppermute | solution.py:37
  25.2 0.0 copy-start
  25.2 1.0 %collective-permute-done.west_ref = bf16[2,8,32,512]{3,2,1,0:T(8,128)(2,1)S(1)} collective-permute-done((bf16[2,8,32,512]{3,2,1,0:T(8,128)(2,1)}, bf16[2,8,32,512]{3,2,1,0:T(8,128)(2,1)S(1)}, u32[]{:S(2)}, u32[]{:S(2)}) %collective-permute-start) | collective-permute-done | bytes 524320 | tf_op jit(solution)/shard_map/ppermute | solution.py:41
  26.2 2.5 %collective-permute-done.1.east_ref = bf16[2,8,32,512]{3,2,1,0:T(8,128)(2,1)S(1)} collective-permute-done((bf16[2,8,32,512]{3,2,1,0:T(8,128)(2,1)}, bf16[2,8,32,512]{3,2,1,0:T(8,128)(2,1)S(1)}, u32[]{:S(2)}, u32[]{:S(2)}) %collective-permute-start.1) | collective-permute-done | bytes 524320 | tf_op jit(solution)/shard_map/ppermute | solution.py:41
  28.8 0.0 copy-done
  28.8 0.0 copy-done.3
  28.8 0.0 copy-start.4
  28.8 0.8 %copy-done.4 = bf16[2,8,32,512]{3,2,1,0:T(8,128)(2,1)} copy-done((bf16[2,8,32,512]{3,2,1,0:T(8,128)(2,1)}, bf16[2,8,32,512]{3,2,1,0:T(8,128)(2,1)S(1)}, u32[]{:S(2)}) %copy-start.4) | copy-done | bytes 524312
  29.6 16.6 %shard_map.94 = (bf16[8,48,512]{2,1,0:T(8,128)(2,1)}, bf16[8,48,512]{2,1,0:T(8,128)(2,1)}, f32[2,8,48,512]{3,2,1,0:T(8,128)}, bf16[2,8,32,512]{3,2,1,0:T(8,128)(...) custom-call(s32[2]{0:T(128)} %pad_add_fusion.here_ref, ...), custom_call_target="tpu_custom_call" | custom-call | tf_op jit(solution)/shard_map/pallas_call | solution.py:220
  46.2 0.0 copy-start.7
  46.2 0.0 copy-start.6
  46.2 1.3 %collective-permute-start.8 = (bf16[8,2,16,512]{3,2,1,0:T(8,128)(2,1)}, bf16[8,2,16,512]{3,2,1,0:T(8,128)(2,1)S(1)}, u32[]{:S(2)}, u32[]{:S(2)}) collective-permute-start(bf16[8,2,16,512]{3,2,1,0:T(8,128)(2,1)} %get-tuple-element.25), channel_id=1, source_target_pairs={{0,16},{16,0},{32,48},{48,32},{64,80},{80,64},{96,112},{112,96},{1... | collective-permute-start | bytes 786440 | tf_op jit(solution)/shard_map/ppermute | solution.py:37
  47.5 1.4 %collective-permute-done.8 = bf16[8,2,16,512]{3,2,1,0:T(8,128)(2,1)S(1)} collective-permute-done((bf16[8,2,16,512]{3,2,1,0:T(8,128)(2,1)}, bf16[8,2,16,512]{3,2,1,0:T(8,128)(2,1)S(1)}, u32[]{:S(2)}, u32[]{:S(2)}) %collective-permute-start.8) | collective-permute-done | bytes 262176 | tf_op jit(solution)/shard_map/ppermute | solution.py:37
  48.8 1.1 %convert_add_fusion = f32[8,2,16,512]{3,2,1,0:T(8,128)S(1)} fusion(f32[8,2,16,512]{3,2,1,0:T(8,128)} %get-tuple-element.24, bf16[8,2,16,512]{3,2,1,0:T(8,128)(2,1)S(1)} %collective-permute-done.8), kind=kLoop, calls=%fused_computation | loop fusion | flops 262144 | bytes 1310720 | tf_op jit(solution)/shard_map/add | solution.py:283
  50.0 0.1 collective-permute-start.9
  50.1 0.0 copy-done.7
  50.1 2.0 %collective-permute-start.6 = (bf16[2,8,32,512]{3,2,1,0:T(8,128)(2,1)S(1)}, bf16[2,8,32,512]{3,2,1,0:T(8,128)(2,1)S(1)}, u32[]{:S(2)}, u32[]{:S(2)}) collective-permute-start(bf16[2,8,32,512]{3,2,1,0:T(8,128)(2,1)S(1)} %copy-done.7), channel_id=1, source_target_pairs={{0,16},{16,32},{32,48},{48,64},{64,80},{80,96},{96,112},{112,128},... | collective-permute-start | bytes 1572872 | tf_op jit(solution)/shard_map/ppermute | solution.py:41
  52.1 0.0 copy-done.6
  52.1 0.0 collective-permute-start.7
  52.1 2.7 %collective-permute-done.9 = bf16[4,2,16,512]{3,2,1,0:T(8,128)(2,1)S(1)} collective-permute-done((bf16[4,2,16,512]{3,2,1,0:T(8,128)(2,1)S(1)}, bf16[4,2,16,512]{3,2,1,0:T(8,128)(2,1)S(1)}, u32[]{:S(2)}, u32[]{:S(2)}) %collective-permute-start.9) | collective-permute-done | bytes 131104 | tf_op jit(solution)/shard_map/ppermute | solution.py:37
  54.8 3.1 %collective-permute-start.10 = (bf16[2,2,16,512]{3,2,1,0:T(8,128)(2,1)S(1)}, bf16[2,2,16,512]{3,2,1,0:T(8,128)(2,1)S(1)}, u32[]{:S(2)}, u32[]{:S(2)}) collective-permute-start(bf16[2,2,16,512]{3,2,1,0:T(8,128)(2,1)S(1)} %slice.39), channel_id=1, source_target_pairs={{0,64},{16,80},{32,96},{48,112},{64,0},{80,16},{96,32},{112,48},{1... | collective-permute-start | bytes 196616 | tf_op jit(solution)/shard_map/ppermute | solution.py:37
  58.0 6.9 %collective-permute-done.10 = bf16[2,2,16,512]{3,2,1,0:T(8,128)(2,1)S(1)} collective-permute-done((bf16[2,2,16,512]{3,2,1,0:T(8,128)(2,1)S(1)}, bf16[2,2,16,512]{3,2,1,0:T(8,128)(2,1)S(1)}, u32[]{:S(2)}, u32[]{:S(2)}) %collective-permute-start.10) | collective-permute-done | bytes 65568 | tf_op jit(solution)/shard_map/ppermute | solution.py:37
  64.9 0.6 collective-permute-start.11
  65.5 0.6 slice.31.keep_ref
  66.1 1.6 %collective-permute-done.11.cap_ref = bf16[1,2,16,512]{3,2,1,0:T(8,128)(2,1)S(1)} collective-permute-done((bf16[1,2,16,512]{3,2,1,0:T(8,128)(2,1)S(1)}, bf16[1,2,16,512]{3,2,1,0:T(8,128)(2,1)S(1)}, u32[]{:S(2)}, u32[]{:S(2)}) %collective-permute-start.11) | collective-permute-done | bytes 32800 | tf_op jit(solution)/shard_map/ppermute | solution.py:37
  67.7 0.0 copy-start.5
  67.7 0.0 collective-permute-done.6.west_ref
  67.7 0.0 collective-permute-done.7.east_ref
  67.7 0.0 copy-start.2
  67.8 0.6 copy-done.5
  68.4 0.2 copy-done.1
  68.6 0.2 copy-done.2
  68.7 2.8 %shard_map.95 = (bf16[8,48,512]{2,1,0:T(8,128)(2,1)}, bf16[8,48,512]{2,1,0:T(8,128)(2,1)}) custom-call(s32[2]{0:T(128)} %pad_add_fusion.here_ref, s32[16]{0:T(128)} %cap_blocks_ref.3, f32[2,8,48,512]{3,2,1,0:T(8,128)} %get-tuple-element.21.own_ref, bf16[2,8,32,512]{3,2,1,0:T(8,128)(2,1)} %copy-done.1, bf16[2,8,32,512]{3,2,1,0:T(8,128)(2,1)} %copy-done.2, ...), custom_call_target="tpu_custom_call" | custom-call | tf_op jit(solution)/shard_map/pallas_call | solution.py:260
  (11 shorter events, 0.1 us)
Async XLA Ops:
  3.4 3.6 %collective-permute-start.2 = (bf16[1,2,16,512]{3,2,1,0:T(8,128)(2,1)}, bf16[1,2,16,512]{3,2,1,0:T(8,128)(2,1)S(1)}, u32[]{:S(2)}, u32[]{:S(2)}) collective-permute-start(bf16[1,2,16,512]{3,2,1,0:T(8,128)(2,1)} %get-tuple-element.18), channel_id=1, source_target_pairs={{0,128},{16,144},{32,160},{48,176},{64,192},{80,208},{96,224},{112... | collective-permute-start | bytes 98312 | tf_op jit(solution)/shard_map/ppermute | solution.py:37
  7.8 4.6 %collective-permute-start.3 = (bf16[2,2,16,512]{3,2,1,0:T(8,128)(2,1)S(1)}, bf16[2,2,16,512]{3,2,1,0:T(8,128)(2,1)S(1)}, u32[]{:S(2)}, u32[]{:S(2)}) collective-permute-start(bf16[2,2,16,512]{3,2,1,0:T(8,128)(2,1)S(1)} %pad_maximum_fusion.2), channel_id=1, source_target_pairs={{0,64},{16,80},{32,96},{48,112},{64,0},{80,16},{96,32},{112,48},{1... | collective-permute-start | bytes 196616 | tf_op jit(solution)/shard_map/ppermute | solution.py:37
  13.2 7.4 %collective-permute-start.4 = (bf16[4,2,16,512]{3,2,1,0:T(8,128)(2,1)S(1)}, bf16[4,2,16,512]{3,2,1,0:T(8,128)(2,1)S(1)}, u32[]{:S(2)}, u32[]{:S(2)}) collective-permute-start(bf16[4,2,16,512]{3,2,1,0:T(8,128)(2,1)S(1)} %pad_maximum_fusion.1), channel_id=1, source_target_pairs={{0,32},{16,48},{32,0},{48,16},{64,96},{80,112},{96,64},{112,80},{1... | collective-permute-start | bytes 393224 | tf_op jit(solution)/shard_map/ppermute | solution.py:37
  14.7 11.6 %collective-permute-start = (bf16[2,8,32,512]{3,2,1,0:T(8,128)(2,1)}, bf16[2,8,32,512]{3,2,1,0:T(8,128)(2,1)S(1)}, u32[]{:S(2)}, u32[]{:S(2)}) collective-permute-start(bf16[2,8,32,512]{3,2,1,0:T(8,128)(2,1)} %get-tuple-element.16), channel_id=1, source_target_pairs={{0,16},{16,32},{32,48},{48,64},{64,80},{80,96},{96,112},{112,128},... | collective-permute-start | bytes 1572872 | tf_op jit(solution)/shard_map/ppermute | solution.py:41
  19.8 9.0 %collective-permute-start.1 = (bf16[2,8,32,512]{3,2,1,0:T(8,128)(2,1)}, bf16[2,8,32,512]{3,2,1,0:T(8,128)(2,1)S(1)}, u32[]{:S(2)}, u32[]{:S(2)}) collective-permute-start(bf16[2,8,32,512]{3,2,1,0:T(8,128)(2,1)} %get-tuple-element.17), channel_id=1, source_target_pairs={{0,240},{16,0},{32,16},{48,32},{64,48},{80,64},{96,80},{112,96},{1... | collective-permute-start | bytes 1572872 | tf_op jit(solution)/shard_map/ppermute | solution.py:41
  21.4 3.8 %collective-permute-start.5 = (bf16[8,2,16,512]{3,2,1,0:T(8,128)(2,1)S(1)}, bf16[8,2,16,512]{3,2,1,0:T(8,128)(2,1)S(1)}, u32[]{:S(2)}, u32[]{:S(2)}) collective-permute-start(bf16[8,2,16,512]{3,2,1,0:T(8,128)(2,1)S(1)} %pad_maximum_fusion), channel_id=1, source_target_pairs={{0,16},{16,0},{32,48},{48,32},{64,80},{80,64},{96,112},{112,96},{1... | collective-permute-start | bytes 786440 | tf_op jit(solution)/shard_map/ppermute | solution.py:37
  25.2 3.6 %copy-start = (bf16[16,2,16,512]{3,2,1,0:T(8,128)(2,1)}, bf16[16,2,16,512]{3,2,1,0:T(8,128)(2,1)S(1)}, u32[]{:S(2)}) copy-start(bf16[16,2,16,512]{3,2,1,0:T(8,128)(2,1)S(1)} %constant_dynamic-update-slice_fusion.cap_ref) | copy-start | bytes 1572868
  26.2 2.6 %copy-start.3 = (bf16[2,8,32,512]{3,2,1,0:T(8,128)(2,1)}, bf16[2,8,32,512]{3,2,1,0:T(8,128)(2,1)S(1)}, u32[]{:S(2)}) copy-start(bf16[2,8,32,512]{3,2,1,0:T(8,128)(2,1)S(1)} %collective-permute-done.west_ref) | copy-start | bytes 1572868
  28.8 0.8 %copy-start.4 = (bf16[2,8,32,512]{3,2,1,0:T(8,128)(2,1)}, bf16[2,8,32,512]{3,2,1,0:T(8,128)(2,1)S(1)}, u32[]{:S(2)}) copy-start(bf16[2,8,32,512]{3,2,1,0:T(8,128)(2,1)S(1)} %collective-permute-done.1.east_ref) | copy-start | bytes 1572868
  46.2 3.9 %copy-start.7 = (bf16[2,8,32,512]{3,2,1,0:T(8,128)(2,1)S(1)}, bf16[2,8,32,512]{3,2,1,0:T(8,128)(2,1)}, u32[]{:S(2)}) copy-start(bf16[2,8,32,512]{3,2,1,0:T(8,128)(2,1)} %get-tuple-element.22) | copy-start | bytes 1572868
  46.2 5.9 %copy-start.6 = (bf16[2,8,32,512]{3,2,1,0:T(8,128)(2,1)S(1)}, bf16[2,8,32,512]{3,2,1,0:T(8,128)(2,1)}, u32[]{:S(2)}) copy-start(bf16[2,8,32,512]{3,2,1,0:T(8,128)(2,1)} %get-tuple-element.23) | copy-start | bytes 1572868
  46.2 2.6 %collective-permute-start.8 = (bf16[8,2,16,512]{3,2,1,0:T(8,128)(2,1)}, bf16[8,2,16,512]{3,2,1,0:T(8,128)(2,1)S(1)}, u32[]{:S(2)}, u32[]{:S(2)}) collective-permute-start(bf16[8,2,16,512]{3,2,1,0:T(8,128)(2,1)} %get-tuple-element.25), channel_id=1, source_target_pairs={{0,16},{16,0},{32,48},{48,32},{64,80},{80,64},{96,112},{112,96},{1... | collective-permute-start | bytes 786440 | tf_op jit(solution)/shard_map/ppermute | solution.py:37
  50.0 4.8 %collective-permute-start.9 = (bf16[4,2,16,512]{3,2,1,0:T(8,128)(2,1)S(1)}, bf16[4,2,16,512]{3,2,1,0:T(8,128)(2,1)S(1)}, u32[]{:S(2)}, u32[]{:S(2)}) collective-permute-start(bf16[4,2,16,512]{3,2,1,0:T(8,128)(2,1)S(1)} %slice.38), channel_id=1, source_target_pairs={{0,32},{16,48},{32,0},{48,16},{64,96},{80,112},{96,64},{112,80},{1... | collective-permute-start | bytes 393224 | tf_op jit(solution)/shard_map/ppermute | solution.py:37
  50.1 17.6 %collective-permute-start.6 = (bf16[2,8,32,512]{3,2,1,0:T(8,128)(2,1)S(1)}, bf16[2,8,32,512]{3,2,1,0:T(8,128)(2,1)S(1)}, u32[]{:S(2)}, u32[]{:S(2)}) collective-permute-start(bf16[2,8,32,512]{3,2,1,0:T(8,128)(2,1)S(1)} %copy-done.7), channel_id=1, source_target_pairs={{0,16},{16,32},{32,48},{48,64},{64,80},{80,96},{96,112},{112,128},... | collective-permute-start | bytes 1572872 | tf_op jit(solution)/shard_map/ppermute | solution.py:41
  52.1 15.7 %collective-permute-start.7 = (bf16[2,8,32,512]{3,2,1,0:T(8,128)(2,1)S(1)}, bf16[2,8,32,512]{3,2,1,0:T(8,128)(2,1)S(1)}, u32[]{:S(2)}, u32[]{:S(2)}) collective-permute-start(bf16[2,8,32,512]{3,2,1,0:T(8,128)(2,1)S(1)} %copy-done.6), channel_id=1, source_target_pairs={{0,240},{16,0},{32,16},{48,32},{64,48},{80,64},{96,80},{112,96},{1... | collective-permute-start | bytes 1572872 | tf_op jit(solution)/shard_map/ppermute | solution.py:41
  54.8 10.0 %collective-permute-start.10 = (bf16[2,2,16,512]{3,2,1,0:T(8,128)(2,1)S(1)}, bf16[2,2,16,512]{3,2,1,0:T(8,128)(2,1)S(1)}, u32[]{:S(2)}, u32[]{:S(2)}) collective-permute-start(bf16[2,2,16,512]{3,2,1,0:T(8,128)(2,1)S(1)} %slice.39), channel_id=1, source_target_pairs={{0,64},{16,80},{32,96},{48,112},{64,0},{80,16},{96,32},{112,48},{1... | collective-permute-start | bytes 196616 | tf_op jit(solution)/shard_map/ppermute | solution.py:37
  64.9 2.9 %collective-permute-start.11 = (bf16[1,2,16,512]{3,2,1,0:T(8,128)(2,1)S(1)}, bf16[1,2,16,512]{3,2,1,0:T(8,128)(2,1)S(1)}, u32[]{:S(2)}, u32[]{:S(2)}) collective-permute-start(bf16[1,2,16,512]{3,2,1,0:T(8,128)(2,1)S(1)} %slice.40), channel_id=1, source_target_pairs={{0,128},{16,144},{32,160},{48,176},{64,192},{80,208},{96,224},{112... | collective-permute-start | bytes 98312 | tf_op jit(solution)/shard_map/ppermute | solution.py:37
  67.7 0.6 copy-start.5
  67.7 0.8 %copy-start.1 = (bf16[2,8,32,512]{3,2,1,0:T(8,128)(2,1)}, bf16[2,8,32,512]{3,2,1,0:T(8,128)(2,1)S(1)}, u32[]{:S(2)}) copy-start(bf16[2,8,32,512]{3,2,1,0:T(8,128)(2,1)S(1)} %collective-permute-done.6.west_ref) | copy-start | bytes 1572868
  67.7 1.0 %copy-start.2 = (bf16[2,8,32,512]{3,2,1,0:T(8,128)(2,1)}, bf16[2,8,32,512]{3,2,1,0:T(8,128)(2,1)S(1)}, u32[]{:S(2)}) copy-start(bf16[2,8,32,512]{3,2,1,0:T(8,128)(2,1)S(1)} %collective-permute-done.7.east_ref) | copy-start | bytes 1572868

commit v2 on v1

v2 whole, which is shorter than its diff:
```python
import jax
import jax.numpy as jnp
from jax import lax
from jax.experimental import pallas as pl
from jax.experimental.pallas import tpu as pltpu
from jax.sharding import PartitionSpec as P

HSIZE = 64
BR = 8
BC = 16
NB = 3
HALO = 2
BANDS = 8
HD = 512
PAIR = 2 * HSIZE
PAIRS = HD // PAIR
TOK = BR * BC
ROWS2 = 2 * TOK
LON = 16
CAPK = LON * BC
RIM = HALO * BC
FAR = -1e30
SCALE = HSIZE**-0.5
XMASKS, YMASK, CMASK = (2, 4, 6), 8, 1
VMEM = 32 * 1024 * 1024
F32 = jnp.float32
BF16 = jnp.bfloat16
RIMS = (((0, 0, 2), (0, 1, 1)), ((0, 1, 2), (1, 0, 2)), ((1, 0, 1), (1, 1, 2)))


def swap(value, mask):
    return lax.ppermute(value, "lon", [(i, i ^ mask) for i in range(LON)])


def shift(value, steps):
    return lax.ppermute(value, "lon", [(i, (i + steps) % LON) for i in range(LON)])


def nt(left, right):
    return lax.dot_general(left, right, (((1,), (1,)), ((), ())), preferred_element_type=F32)


def nn(left, right):
    return lax.dot_general(left, right, (((1,), (0,)), ((), ())), preferred_element_type=F32)


def anywhere(count):
    return [pl.BlockSpec(memory_space=pl.ANY)] * count


def smem():
    return pl.BlockSpec(memory_space=pltpu.SMEM)


def cost(microseconds):
    return pl.CostEstimate(
        flops=0, bytes_accessed=int(microseconds * 3.5e6), transcendentals=0
    )


def lane_blocks(shape):
    return ("lanes", shape)


def stat_blocks():
    return ("lead", (PAIRS, 16, ROWS2))


def turn_blocks():
    return ("lead", (PAIRS, NB, PAIR, TOK))


STATS = jax.ShapeDtypeStruct((PAIRS, 16, ROWS2), F32)
TURNS = jax.ShapeDtypeStruct((PAIRS, NB, PAIR, TOK), F32)
GRID = (BR, NB * BC, HD)
RIM_SHAPE = (2, BR, RIM, HD)
CAP_SHAPE = (LON, 2, BC, HD)
HALF_SHAPE = (LON // 2, 2, BC, HD)


def call(kernel, us, ins, outs, out_shape, operands, part=(0, 1), into=(), behind=()):
    index, count = part
    many = isinstance(out_shape, tuple)
    kinds = list(ins) + (list(outs) if many else [outs])
    inputs = len(ins)

    def view(kind, ref, pair):
        if not isinstance(kind, tuple):
            return ref
        name, shape = kind
        if name == "lead":
            return ref.at[pl.ds(pair, 1)]
        return ref.at[(slice(None),) * (len(shape) - 1) + (pl.ds(pair * PAIR, PAIR),)]

    def whole(*refs):
        refs = refs[:inputs] + refs[inputs + len(into) + len(behind) :]
        for pair in range(PAIRS // count):
            kernel(*[view(kind, ref, pair) for kind, ref in zip(kinds, refs)])

    def spec(kind):
        if not isinstance(kind, tuple):
            return kind
        name, shape = kind
        zeros = (0,) * (len(shape) - 1)
        if name == "lead":
            return pl.BlockSpec((shape[0] // count,) + shape[1:], lambda p: (index,) + zeros)
        return pl.BlockSpec(shape[:-1] + (shape[-1] // count,), lambda p: zeros + (index,))

    specs = [spec(kind) for kind in kinds]
    return pl.pallas_call(
        whole,
        out_shape=out_shape,
        grid=(1,),
        in_specs=specs[:inputs] + anywhere(len(into) + len(behind)),
        out_specs=tuple(specs[inputs:]) if many else specs[-1],
        input_output_aliases={inputs + n: n for n in range(len(into))},
        cost_estimate=cost(us),
        compiler_params=pltpu.CompilerParams(vmem_limit_bytes=VMEM),
    )(*operands, *into, *behind)


def after(value, *others):
    return pl.pallas_call(
        lambda *refs: None,
        out_shape=jax.ShapeDtypeStruct(value.shape, value.dtype),
        in_specs=anywhere(1 + len(others)),
        out_specs=anywhere(1)[0],
        input_output_aliases={0: 0},
        cost_estimate=cost(0.1),
        compiler_params=pltpu.CompilerParams(vmem_limit_bytes=1024 * 1024),
    )(value, *others)


def held(*values):
    return pl.pallas_call(
        lambda *refs: None,
        out_shape=tuple(jax.ShapeDtypeStruct(value.shape, value.dtype) for value in values),
        in_specs=anywhere(len(values)),
        out_specs=tuple(anywhere(len(values))),
        input_output_aliases={n: n for n in range(len(values))},
        cost_estimate=cost(0.1),
        compiler_params=pltpu.CompilerParams(vmem_limit_bytes=1024 * 1024),
    )(*values)


def pole_row(lat):
    return jnp.where(lat == 0, 0, BR - 1)


def edges_kernel(cap_blocks_ref, k_ref, v_ref, cap_ref, east_ref, west_ref, sems):
    row = pole_row(lax.axis_index("lat"))
    column = pl.multiple_of(cap_blocks_ref[lax.axis_index("lon")] * BC, BC)
    copies = []
    for n, ref in enumerate((k_ref, v_ref)):
        pairs = (
            (ref.at[row, pl.ds(column, BC), :], cap_ref.at[0, n]),
            (ref.at[:, pl.ds(NB * BC - RIM, RIM), :], east_ref.at[n]),
            (ref.at[:, pl.ds(0, RIM), :], west_ref.at[n]),
        )
        for m, (source, target) in enumerate(pairs):
            copies.append(pltpu.make_async_copy(source, target, sems.at[3 * n + m]))
    for copy in copies:
        copy.start()
    for copy in copies:
        copy.wait()


def block_of(ref, prefix, column):
    return ref[prefix + (slice(None), pl.ds(column, BC), slice(None))].reshape(TOK, PAIR)


def masked_heads(block):
    lane = lax.broadcasted_iota(jnp.int32, block.shape, 1)
    zero = jnp.zeros_like(block)
    return jnp.concatenate(
        [jnp.where(lane < HSIZE, block, zero), jnp.where(lane < HSIZE, zero, block)], axis=0
    )


def query_rows(q_ref, i):
    return masked_heads(block_of(q_ref, (), i * BC) * jnp.asarray(SCALE, BF16))


def grad_rows(d_ref, i):
    return masked_heads(block_of(d_ref, (), i * BC))


def own_rows(ref):
    return jnp.concatenate([block_of(ref, (), j * BC) for j in range(NB)], axis=0)


def rim_rows(sides, n, i):
    return jnp.concatenate(
        [block_of(sides[side], (n,), block * BC) for side, block, _ in RIMS[i]], axis=0
    )


def cap_rows(cap_ref, n):
    return cap_ref[:, n].reshape(CAPK, PAIR)


def far(width, distance):
    return jnp.where(distance <= width, 0.0, FAR).astype(F32)


def cap_bias():
    lat = lax.axis_index("lat")
    return jnp.where((lat == 0) | (lat == BANDS - 1), 0.0, FAR).astype(F32)


def pieces(value):
    return [value[n * TOK : (n + 1) * TOK] for n in range(value.shape[0] // TOK)]


def column_top(scores, biases):
    tops = [s.max(0, keepdims=True) + b for s, b in zip(scores, biases)]
    top = tops[0]
    for other in tops[1:]:
        top = jnp.maximum(top, other)
    return top


def merged(scores, grads, biases, stats=None):
    top = column_top(scores, biases)
    if stats is not None:
        top = jnp.maximum(top, stats[0])
    weights = [jnp.exp(s - (top - b)) for s, b in zip(scores, biases)]
    total = sum(w.sum(0, keepdims=True) for w in weights)
    dot = sum((w * g).sum(0, keepdims=True) for w, g in zip(weights, grads))
    if stats is not None:
        fade = jnp.exp(stats[0] - top)
        total, dot = total + stats[1] * fade, dot + stats[2] * fade
    return weights, (top, total, dot)


def read_stats(ref, i):
    return tuple(ref[0, 3 * i + n : 3 * i + n + 1, :] for n in range(3))


def write_stats(ref, i, stats):
    for n, value in enumerate(stats):
        ref[0, 3 * i + n : 3 * i + n + 1, :] = value


def slopes_of(keys, values, query, grad, biases, stats):
    top, inverse, dot = stats
    weights, slopes = [], []
    for s, g, b in zip(pieces(nt(keys, query)), pieces(nt(values, grad)), biases):
        weight = jnp.exp(s - (top - b)) * inverse
        slopes.append((weight * (g - dot)).astype(BF16))
        weights.append(weight.astype(BF16))
    return jnp.concatenate(weights, axis=0), jnp.concatenate(slopes, axis=0)


def own_stats_kernel(width_ref, q_ref, k_ref, v_ref, d_ref, stats_ref):
    width = width_ref[lax.axis_index("lat")]
    keys, values = own_rows(k_ref), own_rows(v_ref)
    for i in range(NB):
        biases = [far(width, abs(j - i)) for j in range(NB)]
        scores = pieces(nt(keys, query_rows(q_ref, i)))
        grads = pieces(nt(values, grad_rows(d_ref, i)))
        write_stats(stats_ref, i, merged(scores, grads, biases)[1])


def rim_stats_kernel(width_ref, q_ref, d_ref, west_ref, east_ref, old_ref, stats_ref):
    width = width_ref[lax.axis_index("lat")]
    sides = (west_ref, east_ref)
    for i in range(NB):
        biases = [far(width, distance) for _, _, distance in RIMS[i]]
        scores = pieces(nt(rim_rows(sides, 0, i), query_rows(q_ref, i)))
        grads = pieces(nt(rim_rows(sides, 1, i), grad_rows(d_ref, i)))
        write_stats(stats_ref, i, merged(scores, grads, biases, read_stats(old_ref, i))[1])


def cap_grads_kernel(q_ref, d_ref, cap_ref, old_ref, stats_ref, keep_ref, send_ref):
    keys, values = cap_rows(cap_ref, 0), cap_rows(cap_ref, 1)
    bias = cap_bias()
    queries = [query_rows(q_ref, i) for i in range(NB)]
    outs = [grad_rows(d_ref, i) for i in range(NB)]
    weights, slopes = [], []
    for i in range(NB):
        scores, grads = nt(keys, queries[i]), nt(values, outs[i])
        (weight,), (top, total, dot) = merged([scores], [grads], [bias], read_stats(old_ref, i))
        inverse = 1.0 / total
        dot = dot * inverse
        write_stats(stats_ref, i, (top, inverse, dot))
        weight = weight * inverse
        slopes.append((weight * (grads - dot)).astype(BF16))
        weights.append(weight.astype(BF16))
    pairs = ((slopes, queries), (weights, outs))
    for n, (lefts, rights) in enumerate(pairs):
        value = nn(jnp.concatenate(lefts, axis=1), jnp.concatenate(rights, axis=0))
        value = value.reshape(LON, BC, PAIR)
        keep_ref[:, n] = value[: LON // 2]
        send_ref[:, n] = value[LON // 2 :].astype(BF16)


def heads_of(value):
    return jnp.concatenate([value[:HSIZE, :TOK], value[HSIZE:, TOK:]], axis=0)


def rim_grads_kernel(
    width_ref, q_ref, d_ref, west_ref, east_ref, stats_ref, to_west_ref, to_east_ref, ot_ref, qt_ref
):
    width = width_ref[lax.axis_index("lat")]
    sides, outs = (west_ref, east_ref), (to_west_ref, to_east_ref)
    sums = {}
    for i in range(NB):
        biases = [far(width, distance) for _, _, distance in RIMS[i]]
        query, grad = query_rows(q_ref, i), grad_rows(d_ref, i)
        keys, values = rim_rows(sides, 0, i), rim_rows(sides, 1, i)
        weights, slopes = slopes_of(keys, values, query, grad, biases, read_stats(stats_ref, i))
        ot_ref[0, i] = heads_of(nn(values.T, weights))
        qt_ref[0, i] = heads_of(nn(keys.T, slopes))
        for n, value in enumerate((nn(slopes, query), nn(weights, grad))):
            for piece, (side, block, _) in zip(pieces(value), RIMS[i]):
                key = (n, side, block)
                sums[key] = sums[key] + piece if key in sums else piece
    for (n, side, block), value in sums.items():
        outs[side][n, :, block * BC : (block + 1) * BC, :] = value.astype(BF16).reshape(
            BR, BC, PAIR
        )


def own_grads_kernel(
    width_ref,
    q_ref,
    k_ref,
    v_ref,
    d_ref,
    cap_ref,
    stats_ref,
    ot_ref,
    qt_ref,
    o_ref,
    dq_ref,
    own_ref,
):
    width = width_ref[lax.axis_index("lat")]
    bias = cap_bias()
    keys = jnp.concatenate([own_rows(k_ref), cap_rows(cap_ref, 0)], axis=0)
    values = jnp.concatenate([own_rows(v_ref), cap_rows(cap_ref, 1)], axis=0)
    keys_turned, values_turned = keys.T, values.T
    count = NB * TOK
    sums = [None, None]
    for i in range(NB):
        biases = [far(width, abs(j - i)) for j in range(NB)] + [bias] * (CAPK // TOK)
        query, grad = query_rows(q_ref, i), grad_rows(d_ref, i)
        weights, slopes = slopes_of(keys, values, query, grad, biases, read_stats(stats_ref, i))
        out = ot_ref[0, i] + heads_of(nn(values_turned, weights))
        turn = (qt_ref[0, i] + heads_of(nn(keys_turned, slopes))) * SCALE
        for ref, value in ((o_ref, out), (dq_ref, turn)):
            ref[:, i * BC : (i + 1) * BC, :] = value.T.astype(BF16).reshape(BR, BC, PAIR)
        for n, value in enumerate((nn(slopes[:count], query), nn(weights[:count], grad))):
            sums[n] = value if sums[n] is None else sums[n] + value
    for n, value in enumerate(sums):
        for j, piece in enumerate(pieces(value)):
            own_ref[n, :, j * BC : (j + 1) * BC, :] = piece.reshape(BR, BC, PAIR)


def join_kernel(
    cap_blocks_ref, own_ref, west_ref, east_ref, keep_ref, *refs
):
    row = pole_row(lax.axis_index("lat"))
    column = pl.multiple_of(cap_blocks_ref[lax.axis_index("lon")] * BC, BC)
    caps, (dk_ref, dv_ref, total) = refs[:-3], refs[-3:]
    for n, ref in enumerate((dk_ref, dv_ref)):
        total[...] = own_ref[n]
        total[:, :RIM, :] += west_ref[n].astype(F32)
        total[:, NB * BC - RIM :, :] += east_ref[n].astype(F32)
        total[row, pl.ds(column, BC), :] += keep_ref[0, n] + sum(
            ref[0, n].astype(F32) for ref in caps
        )
        ref[...] = total[...].astype(BF16)


def shards(query, keys, values, grad_out, band_width, cap_blocks):
    grid = jax.ShapeDtypeStruct(GRID, BF16)
    rim = jax.ShapeDtypeStruct(RIM_SHAPE, BF16)
    keys, values, query, grad_out = held(keys, values, query, grad_out)
    cap, to_east, to_west = pl.pallas_call(
        edges_kernel,
        out_shape=(jax.ShapeDtypeStruct((1, 2, BC, HD), BF16), rim, rim),
        in_specs=[smem()] + anywhere(2),
        out_specs=tuple(anywhere(3)),
        scratch_shapes=[pltpu.SemaphoreType.DMA((6,))],
        cost_estimate=cost(1),
        compiler_params=pltpu.CompilerParams(vmem_limit_bytes=1024 * 1024),
    )(cap_blocks, keys, values)
    west = shift(to_east, 1)
    east = shift(to_west, -1)

    g, r, w = lane_blocks(GRID), lane_blocks(RIM_SHAPE), lane_blocks((2,) + GRID)
    c, h = lane_blocks(CAP_SHAPE), lane_blocks(HALF_SHAPE)
    s, t = stat_blocks(), turn_blocks()
    received = swap(cap, YMASK)
    stats = call(
        own_stats_kernel, 0.5, [smem(), g, g, g, g], s, STATS,
        (band_width, query, keys, values, grad_out), behind=(received,),
    )
    cap = jnp.concatenate([cap, received], axis=0)
    cap = jnp.concatenate([cap] + [swap(cap, mask) for mask in XMASKS], axis=0)
    stats = call(
        rim_stats_kernel, 0.5, [smem(), g, g, r, r, s], s, STATS,
        (band_width, query, grad_out, west, east, stats),
    )
    cap = after(cap, stats)
    cap = jnp.concatenate([cap, swap(cap, CMASK)], axis=0)
    stats, keep, send = call(
        cap_grads_kernel, 3, [g, g, c, s], (s, h, h),
        (STATS, jax.ShapeDtypeStruct(HALF_SHAPE, F32), jax.ShapeDtypeStruct(HALF_SHAPE, BF16)),
        (query, grad_out, cap, stats),
    )
    total = keep + swap(send, CMASK).astype(F32)
    total = total.reshape((4, 2) + total.shape[1:])
    keep, send = total[:, 0], total[:, 1].astype(BF16)
    received = swap(send, YMASK)
    to_west, to_east, out_turned, query_turned = call(
        rim_grads_kernel, 4.5, [smem(), g, g, r, r, s], (r, r, t, t),
        (rim, rim, TURNS, TURNS),
        (band_width, query, grad_out, west, east, stats), behind=(keep,),
    )
    from_east = shift(to_west, -1)
    from_west = shift(to_east, 1)

    own_out = (grid, grid, jax.ShapeDtypeStruct((2,) + GRID, F32))
    own_in = (band_width, query, keys, values, grad_out, cap, stats, out_turned, query_turned)

    def own_part(part, into):
        kinds = [smem(), g, g, g, g, c, s, t, t]
        return call(own_grads_kernel, 4, kinds, (g, g, w), own_out, own_in, part, into, (received,))

    first = own_part((0, 2), ())
    total = keep + received.astype(F32)
    keep = total[:1]
    sends = total[1:].astype(BF16)
    caps = [swap(sends[n : n + 1], mask) for n, mask in enumerate(XMASKS)]
    attended, query_grad, own = own_part((1, 2), first)
    v = pl.BlockSpec(memory_space=pltpu.VMEM)
    key_grad, value_grad = pl.pallas_call(
        join_kernel,
        out_shape=(grid, grid),
        in_specs=[smem()] + [v] * (4 + len(caps)),
        out_specs=(v, v),
        scratch_shapes=[pltpu.VMEM(GRID, F32)],
        cost_estimate=cost(2),
        compiler_params=pltpu.CompilerParams(vmem_limit_bytes=VMEM),
    )(cap_blocks, own, from_west, from_east, keep, *caps)
    return attended, query_grad, key_grad, value_grad


def solution(mesh):
    grid = P(("dp", "lat"), "lon", None)
    return jax.shard_map(
        shards,
        mesh=mesh,
        in_specs=(grid, grid, grid, grid, P(), P()),
        out_specs=(grid, grid, grid, grid),
        check_vma=False,
    )
```

time: 72 us -> 51.8 us (0.72)
  the two profiles are of different devices: /device:TPU:1 before, /device:TPU:8 now
where the time goes in v2:
time: 51.8 us; the launch traced here: 51.6 us
  Pallas kernels  23 us (44%)
  starting transfers between devices  19.9 us (38%)
  waiting for transfers between devices  5.03 us (10%)
  local copies, waits for them, and re-layouts  2.77 us (5%)
  between operations  0.83 us (2%)
    pallas_call x6, Pallas kernels, call(): pl.pallas_call(whole, out_shape=out_shape, grid=(1,), in_specs=specs[:inp...  20.6 us
    ppermute x10, starting transfers between devices, swap(): return lax.ppermute(value, 'lon', [(i, i ^ mask) for i in range(LON)])  12.1 us
    ppermute x4, starting transfers between devices, shift(): lax.ppermute(value, 'lon', [(i, (i + steps) % LON) for i in range(LON)])  7.79 us
    ppermute x10, waiting for transfers between devices, swap(): return lax.ppermute(value, 'lon', [(i, i ^ mask) for i in range(LON)])  5.01 us
    unnamed x15, local copies, waits for them, and re-layouts  2.7 us
    pallas_call x1, Pallas kernels, shards(): pl.pallas_call(join_kernel, out_shape=(grid, grid), in_specs=[smem()] + [...  1.65 us
  transfers between devices with their start and end apart: 14, of which 5 were waited for; matrix products, arithmetic and copies ran while one was open for 0% of the time, Pallas kernels for 31%

profile of v2, /device:TPU:8, one launch (start us, length us, event | category | flops | bytes accessed | tf_op | source)
XLA Modules:
  0.0 51.6 jit_solution(6959293913242057133)
XLA Ops:
  0.6 0.0 copy-start.2
  0.6 0.0 copy-start.3
  0.7 1.1 %copy.46.refs_2_ = bf16[8,48,512]{2,1,0:T(8,128)(2,1)S(1)} copy(bf16[8,48,512]{2,1,0:T(8,128)(2,1)} %param.6) | data formatting | bytes 786432
  1.7 1.0 %copy.47.refs_0_ = bf16[8,48,512]{2,1,0:T(8,128)(2,1)S(1)} copy(bf16[8,48,512]{2,1,0:T(8,128)(2,1)} %param.7) | data formatting | bytes 786432
  2.7 0.0 copy-done.2
  2.7 0.0 copy-start.1
  2.7 0.0 copy-done.3
  2.8 0.0 copy-start
  2.8 0.6 %copy-done.1 = s32[16]{0:T(128)S(1)} copy-done((s32[16]{0:T(128)S(1)}, s32[16]{0:T(128)}, u32[]{:S(2)}) %copy-start.1) | copy-done | bytes 88
  3.4 0.7 %shard_map.94 = (bf16[1,2,16,512]{3,2,1,0:T(8,128)(2,1)S(1)}, bf16[2,8,32,512]{3,2,1,0:T(8,128)(2,1)S(1)}, bf16[2,8,32,512]{3,2,1,0:T(8,128)(2,1)S(1)}) custom-call(s32[16]{0:T(128)S(1)} %copy-done.1, bf16[8,48,512]{2,1,0:T(8,128)(2,1)S(1)} %get-tuple-element.27.k_ref.refs_2_, bf16[8,48,512]{2,1,0:T(8,128)(2,1)S(1)} %get-tuple-element.28.v_ref.refs_3_), custom_call_target="tpu_custom_call" | custom-call | bytes 3500000 | tf_op jit(solution)/shard_map/pallas_call | solution.py:381
  4.1 2.3 %collective-permute-start = (bf16[1,2,16,512]{3,2,1,0:T(8,128)(2,1)S(1)}, bf16[1,2,16,512]{3,2,1,0:T(8,128)(2,1)S(1)}, u32[]{:S(2)}, u32[]{:S(2)}) collective-permute-start(bf16[1,2,16,512]{3,2,1,0:T(8,128)(2,1)S(1)} %get-tuple-element.30), channel_id=1, source_target_pairs={{0,128},{16,144},{32,160},{48,176},{64,192},{80,208},{96,224},{112... | collective-permute-start | bytes 98312 | tf_op jit(solution)/shard_map/ppermute | solution.py:32
  6.4 0.0 collective-permute-start.4
  6.4 3.9 %collective-permute-start.5 = (bf16[2,8,32,512]{3,2,1,0:T(8,128)(2,1)S(1)}, bf16[2,8,32,512]{3,2,1,0:T(8,128)(2,1)S(1)}, u32[]{:S(2)}, u32[]{:S(2)}) collective-permute-start(bf16[2,8,32,512]{3,2,1,0:T(8,128)(2,1)S(1)} %get-tuple-element.32), channel_id=1, source_target_pairs={{0,240},{16,0},{32,16},{48,32},{64,48},{80,64},{96,80},{112,96},{1... | collective-permute-start | bytes 1572872 | tf_op jit(solution)/shard_map/ppermute | solution.py:36
  10.3 0.0 collective-permute-done.refs_5_
  10.3 0.1 collective-permute-start.1
  10.4 1.3 %collective-permute-start.3 = (bf16[2,2,16,512]{3,2,1,0:T(8,128)(2,1)S(1)}, bf16[2,2,16,512]{3,2,1,0:T(8,128)(2,1)S(1)}, u32[]{:S(2)}, u32[]{:S(2)}) collective-permute-start(bf16[2,2,16,512]{3,2,1,0:T(8,128)(2,1)S(1)} %get-tuple-element.53), channel_id=1, source_target_pairs={{0,96},{16,112},{32,64},{48,80},{64,32},{80,48},{96,0},{112,16},{1... | collective-permute-start | bytes 196616 | tf_op jit(solution)/shard_map/ppermute | solution.py:32
  11.7 2.7 %collective-permute-start.2 = (bf16[2,2,16,512]{3,2,1,0:T(8,128)(2,1)S(1)}, bf16[2,2,16,512]{3,2,1,0:T(8,128)(2,1)S(1)}, u32[]{:S(2)}, u32[]{:S(2)}) collective-permute-start(bf16[2,2,16,512]{3,2,1,0:T(8,128)(2,1)S(1)} %get-tuple-element.53), channel_id=1, source_target_pairs={{0,64},{16,80},{32,96},{48,112},{64,0},{80,16},{96,32},{112,48},{1... | collective-permute-start | bytes 196616 | tf_op jit(solution)/shard_map/ppermute | solution.py:32
  14.5 0.0 copy-done
  14.5 2.5 %shard_map.95.refs_5_ = f32[4,16,256]{2,1,0:T(8,128)S(1)} custom-call(s32[8]{0:T(128)S(1)} %copy-done, bf16[8,48,512]{2,1,0:T(8,128)(2,1)S(1)} %get-tuple-element.26.refs_1_.refs_0_, bf16[8,48,512]{2,1,0:T(8,128)(2,1)S(1)} %get-tuple-element.27.k_ref.refs_2_, bf16[8,48,512]{2,1,0:T(8,128)(2,1)S(1)} %get-tuple-element.28.v_ref.refs_3_, ...), custom_call_target="tpu_custom_call" | custom-call | bytes 1750000 | tf_op jit(solution)/shard_map/pallas_call | solution.py:110
  17.0 0.2 collective-permute-done.1
  17.2 1.2 %collective-permute-done.2 = bf16[2,2,16,512]{3,2,1,0:T(8,128)(2,1)S(1)} collective-permute-done((bf16[2,2,16,512]{3,2,1,0:T(8,128)(2,1)S(1)}, bf16[2,2,16,512]{3,2,1,0:T(8,128)(2,1)S(1)}, u32[]{:S(2)}, u32[]{:S(2)}) %collective-permute-start.2) | collective-permute-done | bytes 65568 | tf_op jit(solution)/shard_map/ppermute | solution.py:32
  18.4 0.7 %collective-permute-done.3 = bf16[2,2,16,512]{3,2,1,0:T(8,128)(2,1)S(1)} collective-permute-done((bf16[2,2,16,512]{3,2,1,0:T(8,128)(2,1)S(1)}, bf16[2,2,16,512]{3,2,1,0:T(8,128)(2,1)S(1)}, u32[]{:S(2)}, u32[]{:S(2)}) %collective-permute-start.3) | collective-permute-done | bytes 65568 | tf_op jit(solution)/shard_map/ppermute | solution.py:32
  19.1 0.0 collective-permute-done.4.refs_3_
  19.1 0.0 collective-permute-done.5.refs_4_
  19.1 1.9 %shard_map.96.refs_1_.refs_3_ = f32[4,16,256]{2,1,0:T(8,128)S(1)} custom-call(s32[8]{0:T(128)S(1)} %copy-done, bf16[8,48,512]{2,1,0:T(8,128)(2,1)S(1)} %get-tuple-element.26.refs_1_.refs_0_, bf16[8,48,512]{2,1,0:T(8,128)(2,1)S(1)} %get-tuple-element.29.refs_4_.refs_2_.refs_1_, bf16[2,8,32,512]{3,2,1,0:T(8,128)(2,1)S(1)} %collective-permute-done.4.refs_3_, ...), custom_call_target="tpu_custom_call" | custom-call | bytes 1750000 | tf_op jit(solution)/shard_map/pallas_call | solution.py:110
  21.0 0.1 collective-permute-start.6
  21.1 1.5 %collective-permute-done.6 = bf16[8,2,16,512]{3,2,1,0:T(8,128)(2,1)S(1)} collective-permute-done((bf16[8,2,16,512]{3,2,1,0:T(8,128)(2,1)S(1)}, bf16[8,2,16,512]{3,2,1,0:T(8,128)(2,1)S(1)}, u32[]{:S(2)}, u32[]{:S(2)}) %collective-permute-start.6) | collective-permute-done | bytes 262176 | tf_op jit(solution)/shard_map/ppermute | solution.py:32
  22.6 2.9 %shard_map.98 = (f32[4,16,256]{2,1,0:T(8,128)S(1)}, f32[8,2,16,512]{3,2,1,0:T(8,128)S(1)}, bf16[8,2,16,512]{3,2,1,0:T(8,128)(2,1)S(1)}) custom-call(bf16[8,48,512]{2,1,0:T(8,128)(2,1)S(1)} %get-tuple-element.26.refs_1_.refs_0_, bf16[8,48,512]{2,1,0:T(8,128)(2,1)S(1)} %get-tuple-element.29.refs_4_.refs_2_.refs_1_, ...), custom_call_target="tpu_custom_call" | custom-call | bytes 10500000 | tf_op jit(solution)/shard_map/pallas_call | solution.py:110
  25.6 0.2 collective-permute-start.7
  25.8 1.4 %collective-permute-done.7 = bf16[8,2,16,512]{3,2,1,0:T(8,128)(2,1)S(1)} collective-permute-done((bf16[8,2,16,512]{3,2,1,0:T(8,128)(2,1)S(1)}, bf16[8,2,16,512]{3,2,1,0:T(8,128)(2,1)S(1)}, u32[]{:S(2)}, u32[]{:S(2)}) %collective-permute-start.7) | collective-permute-done | bytes 262176 | tf_op jit(solution)/shard_map/ppermute | solution.py:32
  27.2 0.1 convert_add_fusion
  27.3 1.2 %collective-permute-start.8 = (bf16[4,2,16,512]{3,2,1,0:T(8,128)(2,1)S(1)}, bf16[4,2,16,512]{3,2,1,0:T(8,128)(2,1)S(1)}, u32[]{:S(2)}, u32[]{:S(2)}) collective-permute-start(bf16[4,2,16,512]{3,2,1,0:T(8,128)(2,1)S(1)} %fusion), channel_id=1, source_target_pairs={{0,128},{16,144},{32,160},{48,176},{64,192},{80,208},{96,224},{112... | collective-permute-start | bytes 393224 | tf_op jit(solution)/shard_map/ppermute | solution.py:32
  28.5 4.5 %shard_map.99 = (bf16[2,8,32,512]{3,2,1,0:T(8,128)(2,1)S(1)}, bf16[2,8,32,512]{3,2,1,0:T(8,128)(2,1)S(1)}, f32[4,3,128,128]{3,2,1,0:T(8,128)S(1)}, f32[4,3,128,128]{3,2,1,0:T(8,128)S(1)}) custom-call(s32[8]{0:T(128)S(1)} %copy-done, bf16[8,48,512]{2,1,0:T(8,128)(2,1)S(1)} %get-tuple-element.26.refs_1_.refs_0_, ...), custom_call_target="tpu_custom_call" | custom-call | bytes 15750000 | tf_op jit(solution)/shard_map/pallas_call | solution.py:110
  33.0 0.2 collective-permute-start.9
  33.1 3.8 %collective-permute-start.10 = (bf16[2,8,32,512]{3,2,1,0:T(8,128)(2,1)S(1)}, bf16[2,8,32,512]{3,2,1,0:T(8,128)(2,1)S(1)}, u32[]{:S(2)}, u32[]{:S(2)}) collective-permute-start(bf16[2,8,32,512]{3,2,1,0:T(8,128)(2,1)S(1)} %get-tuple-element.45), channel_id=1, source_target_pairs={{0,240},{16,0},{32,16},{48,32},{64,48},{80,64},{96,80},{112,96},{1... | collective-permute-start | bytes 1572872 | tf_op jit(solution)/shard_map/ppermute | solution.py:36
  36.9 0.0 collective-permute-done.8.refs_9_.refs_12_
  37.0 1.6 %collective-permute-start.13 = (bf16[1,2,16,512]{3,2,1,0:T(8,128)(2,1)S(1)}, bf16[1,2,16,512]{3,2,1,0:T(8,128)(2,1)S(1)}, u32[]{:S(2)}, u32[]{:S(2)}) collective-permute-start(bf16[1,2,16,512]{3,2,1,0:T(8,128)(2,1)S(1)} %get-tuple-element.50), channel_id=1, source_target_pairs={{0,96},{16,112},{32,64},{48,80},{64,32},{80,48},{96,0},{112,16},{1... | collective-permute-start | bytes 98312 | tf_op jit(solution)/shard_map/ppermute | solution.py:32
  38.5 0.0 collective-permute-start.12
  38.6 2.6 %collective-permute-start.11 = (bf16[1,2,16,512]{3,2,1,0:T(8,128)(2,1)S(1)}, bf16[1,2,16,512]{3,2,1,0:T(8,128)(2,1)S(1)}, u32[]{:S(2)}, u32[]{:S(2)}) collective-permute-start(bf16[1,2,16,512]{3,2,1,0:T(8,128)(2,1)S(1)} %get-tuple-element.52), channel_id=1, source_target_pairs={{0,32},{16,48},{32,0},{48,16},{64,96},{80,112},{96,64},{112,80},{1... | collective-permute-start | bytes 98312 | tf_op jit(solution)/shard_map/ppermute | solution.py:32
  41.1 4.4 %shard_map.100 = (bf16[8,48,512]{2,1,0:T(8,128)(2,1)}, bf16[8,48,512]{2,1,0:T(8,128)(2,1)}, f32[2,8,48,512]{3,2,1,0:T(8,128)S(1)}) custom-call(s32[8]{0:T(128)S(1)} %copy-done, bf16[8,48,512]{2,1,0:T(8,128)(2,1)S(1)} %get-tuple-element.26.refs_1_.refs_0_, bf16[8,48,512]{2,1,0:T(8,128)(2,1)S(1)} %get-tuple-element.27.k_ref.refs_2_, ...), custom_call_target="tpu_custom_call" | custom-call | bytes 14000000 | tf_op jit(solution)/shard_map/pallas_call | solution.py:110
  45.5 4.4 %shard_map.101 = (bf16[8,48,512]{2,1,0:T(8,128)(2,1)}, bf16[8,48,512]{2,1,0:T(8,128)(2,1)}, f32[2,8,48,512]{3,2,1,0:T(8,128)S(1)}) custom-call(s32[8]{0:T(128)S(1)} %copy-done, bf16[8,48,512]{2,1,0:T(8,128)(2,1)S(1)} %get-tuple-element.26.refs_1_.refs_0_, ...), custom_call_target="tpu_custom_call", output_to_operand_aliasing={{0}: (9, {}), {1}: (10, {}), {2}: (11, {})} | custom-call | bytes 14000000 | tf_op jit(solution)/shard_map/pallas_call | solution.py:110
  49.9 0.0 collective-permute-done.13.refs_2_
  49.9 0.0 collective-permute-done.12.refs_1_
  49.9 0.0 collective-permute-done.11.refs_0_
  50.0 0.0 collective-permute-done.9.west_ref
  50.0 0.0 collective-permute-done.10.east_ref
  50.0 1.7 %shard_map.102 = (bf16[8,48,512]{2,1,0:T(8,128)(2,1)}, bf16[8,48,512]{2,1,0:T(8,128)(2,1)}) custom-call(s32[16]{0:T(128)S(1)} %copy-done.1, f32[2,8,48,512]{3,2,1,0:T(8,128)S(1)} %get-tuple-element.43.own_ref, bf16[2,8,32,512]{3,2,1,0:T(8,128)(2,1)S(1)} %collective-permute-done.9.west_ref, bf16[2,8,32,512]{3,2,1,0:T(8,128)(2,1)S(1)} %collective-permute-done.10.east_ref, ...), custom_call_target="tpu_custom_call" | custom-call | bytes 7000000 | tf_op jit(solution)/shard_map/pallas_call | solution.py:440
  (15 shorter events, 0.2 us)
Async XLA Ops:
  0.6 2.1 %copy-start.2 = (bf16[8,48,512]{2,1,0:T(8,128)(2,1)S(1)}, bf16[8,48,512]{2,1,0:T(8,128)(2,1)}, u32[]{:S(2)}) copy-start(bf16[8,48,512]{2,1,0:T(8,128)(2,1)} %param.8) | copy-start | bytes 1179652
  0.6 2.1 %copy-start.3 = (bf16[8,48,512]{2,1,0:T(8,128)(2,1)S(1)}, bf16[8,48,512]{2,1,0:T(8,128)(2,1)}, u32[]{:S(2)}) copy-start(bf16[8,48,512]{2,1,0:T(8,128)(2,1)} %param.9) | copy-start | bytes 1179652
  2.7 0.7 %copy-start.1 = (s32[16]{0:T(128)S(1)}, s32[16]{0:T(128)}, u32[]{:S(2)}) copy-start(s32[16]{0:T(128)} %cap_blocks_ref.3) | copy-start | bytes 196
  2.8 11.7 %copy-start = (s32[8]{0:T(128)S(1)}, s32[8]{0:T(128)}, u32[]{:S(2)}) copy-start(s32[8]{0:T(128)} %refs_0_.10) | copy-start | bytes 100
  4.1 6.1 %collective-permute-start = (bf16[1,2,16,512]{3,2,1,0:T(8,128)(2,1)S(1)}, bf16[1,2,16,512]{3,2,1,0:T(8,128)(2,1)S(1)}, u32[]{:S(2)}, u32[]{:S(2)}) collective-permute-start(bf16[1,2,16,512]{3,2,1,0:T(8,128)(2,1)S(1)} %get-tuple-element.30), channel_id=1, source_target_pairs={{0,128},{16,144},{32,160},{48,176},{64,192},{80,208},{96,224},{112... | collective-permute-start | bytes 98312 | tf_op jit(solution)/shard_map/ppermute | solution.py:32
  6.4 12.7 %collective-permute-start.4 = (bf16[2,8,32,512]{3,2,1,0:T(8,128)(2,1)S(1)}, bf16[2,8,32,512]{3,2,1,0:T(8,128)(2,1)S(1)}, u32[]{:S(2)}, u32[]{:S(2)}) collective-permute-start(bf16[2,8,32,512]{3,2,1,0:T(8,128)(2,1)S(1)} %get-tuple-element.31), channel_id=1, source_target_pairs={{0,16},{16,32},{32,48},{48,64},{64,80},{80,96},{96,112},{112,128},... | collective-permute-start | bytes 1572872 | tf_op jit(solution)/shard_map/ppermute | solution.py:36
  6.4 12.7 %collective-permute-start.5 = (bf16[2,8,32,512]{3,2,1,0:T(8,128)(2,1)S(1)}, bf16[2,8,32,512]{3,2,1,0:T(8,128)(2,1)S(1)}, u32[]{:S(2)}, u32[]{:S(2)}) collective-permute-start(bf16[2,8,32,512]{3,2,1,0:T(8,128)(2,1)S(1)} %get-tuple-element.32), channel_id=1, source_target_pairs={{0,240},{16,0},{32,16},{48,32},{64,48},{80,64},{96,80},{112,96},{1... | collective-permute-start | bytes 1572872 | tf_op jit(solution)/shard_map/ppermute | solution.py:36
  10.3 6.9 %collective-permute-start.1 = (bf16[2,2,16,512]{3,2,1,0:T(8,128)(2,1)S(1)}, bf16[2,2,16,512]{3,2,1,0:T(8,128)(2,1)S(1)}, u32[]{:S(2)}, u32[]{:S(2)}) collective-permute-start(bf16[2,2,16,512]{3,2,1,0:T(8,128)(2,1)S(1)} %get-tuple-element.53), channel_id=1, source_target_pairs={{0,32},{16,48},{32,0},{48,16},{64,96},{80,112},{96,64},{112,80},{1... | collective-permute-start | bytes 196616 | tf_op jit(solution)/shard_map/ppermute | solution.py:32
  10.4 8.7 %collective-permute-start.3 = (bf16[2,2,16,512]{3,2,1,0:T(8,128)(2,1)S(1)}, bf16[2,2,16,512]{3,2,1,0:T(8,128)(2,1)S(1)}, u32[]{:S(2)}, u32[]{:S(2)}) collective-permute-start(bf16[2,2,16,512]{3,2,1,0:T(8,128)(2,1)S(1)} %get-tuple-element.53), channel_id=1, source_target_pairs={{0,96},{16,112},{32,64},{48,80},{64,32},{80,48},{96,0},{112,16},{1... | collective-permute-start | bytes 196616 | tf_op jit(solution)/shard_map/ppermute | solution.py:32
  11.7 6.6 %collective-permute-start.2 = (bf16[2,2,16,512]{3,2,1,0:T(8,128)(2,1)S(1)}, bf16[2,2,16,512]{3,2,1,0:T(8,128)(2,1)S(1)}, u32[]{:S(2)}, u32[]{:S(2)}) collective-permute-start(bf16[2,2,16,512]{3,2,1,0:T(8,128)(2,1)S(1)} %get-tuple-element.53), channel_id=1, source_target_pairs={{0,64},{16,80},{32,96},{48,112},{64,0},{80,16},{96,32},{112,48},{1... | collective-permute-start | bytes 196616 | tf_op jit(solution)/shard_map/ppermute | solution.py:32
  21.0 1.6 %collective-permute-start.6 = (bf16[8,2,16,512]{3,2,1,0:T(8,128)(2,1)S(1)}, bf16[8,2,16,512]{3,2,1,0:T(8,128)(2,1)S(1)}, u32[]{:S(2)}, u32[]{:S(2)}) collective-permute-start(bf16[8,2,16,512]{3,2,1,0:T(8,128)(2,1)S(1)} %shard_map.97), channel_id=1, source_target_pairs={{0,16},{16,0},{32,48},{48,32},{64,80},{80,64},{96,112},{112,96},{1... | collective-permute-start | bytes 786440 | tf_op jit(solution)/shard_map/ppermute | solution.py:32
  25.6 1.6 %collective-permute-start.7 = (bf16[8,2,16,512]{3,2,1,0:T(8,128)(2,1)S(1)}, bf16[8,2,16,512]{3,2,1,0:T(8,128)(2,1)S(1)}, u32[]{:S(2)}, u32[]{:S(2)}) collective-permute-start(bf16[8,2,16,512]{3,2,1,0:T(8,128)(2,1)S(1)} %get-tuple-element.35), channel_id=1, source_target_pairs={{0,16},{16,0},{32,48},{48,32},{64,80},{80,64},{96,112},{112,96},{1... | collective-permute-start | bytes 786440 | tf_op jit(solution)/shard_map/ppermute | solution.py:32
  27.3 9.6 %collective-permute-start.8 = (bf16[4,2,16,512]{3,2,1,0:T(8,128)(2,1)S(1)}, bf16[4,2,16,512]{3,2,1,0:T(8,128)(2,1)S(1)}, u32[]{:S(2)}, u32[]{:S(2)}) collective-permute-start(bf16[4,2,16,512]{3,2,1,0:T(8,128)(2,1)S(1)} %fusion), channel_id=1, source_target_pairs={{0,128},{16,144},{32,160},{48,176},{64,192},{80,208},{96,224},{112... | collective-permute-start | bytes 393224 | tf_op jit(solution)/shard_map/ppermute | solution.py:32
  33.0 17.0 %collective-permute-start.9 = (bf16[2,8,32,512]{3,2,1,0:T(8,128)(2,1)S(1)}, bf16[2,8,32,512]{3,2,1,0:T(8,128)(2,1)S(1)}, u32[]{:S(2)}, u32[]{:S(2)}) collective-permute-start(bf16[2,8,32,512]{3,2,1,0:T(8,128)(2,1)S(1)} %get-tuple-element.44), channel_id=1, source_target_pairs={{0,16},{16,32},{32,48},{48,64},{64,80},{80,96},{96,112},{112,128},... | collective-permute-start | bytes 1572872 | tf_op jit(solution)/shard_map/ppermute | solution.py:36
  33.1 16.8 %collective-permute-start.10 = (bf16[2,8,32,512]{3,2,1,0:T(8,128)(2,1)S(1)}, bf16[2,8,32,512]{3,2,1,0:T(8,128)(2,1)S(1)}, u32[]{:S(2)}, u32[]{:S(2)}) collective-permute-start(bf16[2,8,32,512]{3,2,1,0:T(8,128)(2,1)S(1)} %get-tuple-element.45), channel_id=1, source_target_pairs={{0,240},{16,0},{32,16},{48,32},{64,48},{80,64},{96,80},{112,96},{1... | collective-permute-start | bytes 1572872 | tf_op jit(solution)/shard_map/ppermute | solution.py:36
  37.0 13.0 %collective-permute-start.13 = (bf16[1,2,16,512]{3,2,1,0:T(8,128)(2,1)S(1)}, bf16[1,2,16,512]{3,2,1,0:T(8,128)(2,1)S(1)}, u32[]{:S(2)}, u32[]{:S(2)}) collective-permute-start(bf16[1,2,16,512]{3,2,1,0:T(8,128)(2,1)S(1)} %get-tuple-element.50), channel_id=1, source_target_pairs={{0,96},{16,112},{32,64},{48,80},{64,32},{80,48},{96,0},{112,16},{1... | collective-permute-start | bytes 98312 | tf_op jit(solution)/shard_map/ppermute | solution.py:32
  38.5 11.4 %collective-permute-start.12 = (bf16[1,2,16,512]{3,2,1,0:T(8,128)(2,1)S(1)}, bf16[1,2,16,512]{3,2,1,0:T(8,128)(2,1)S(1)}, u32[]{:S(2)}, u32[]{:S(2)}) collective-permute-start(bf16[1,2,16,512]{3,2,1,0:T(8,128)(2,1)S(1)} %get-tuple-element.51), channel_id=1, source_target_pairs={{0,64},{16,80},{32,96},{48,112},{64,0},{80,16},{96,32},{112,48},{1... | collective-permute-start | bytes 98312 | tf_op jit(solution)/shard_map/ppermute | solution.py:32
  38.6 11.4 %collective-permute-start.11 = (bf16[1,2,16,512]{3,2,1,0:T(8,128)(2,1)S(1)}, bf16[1,2,16,512]{3,2,1,0:T(8,128)(2,1)S(1)}, u32[]{:S(2)}, u32[]{:S(2)}) collective-permute-start(bf16[1,2,16,512]{3,2,1,0:T(8,128)(2,1)S(1)} %get-tuple-element.52), channel_id=1, source_target_pairs={{0,32},{16,48},{32,0},{48,16},{64,96},{80,112},{96,64},{112,80},{1... | collective-permute-start | bytes 98312 | tf_op jit(solution)/shard_map/ppermute | solution.py:32

commit v3 on v2

--- a/solution.py
+++ b/solution.py
@@ -377,7 +377,8 @@
 def shards(query, keys, values, grad_out, band_width, cap_blocks):
     grid = jax.ShapeDtypeStruct(GRID, BF16)
     rim = jax.ShapeDtypeStruct(RIM_SHAPE, BF16)
-    keys, values, query, grad_out = held(keys, values, query, grad_out)
+    keys, values = held(keys, values)
+    query, grad_out = held(query, grad_out)
     cap, to_east, to_west = pl.pallas_call(
         edges_kernel,
         out_shape=(jax.ShapeDtypeStruct((1, 2, BC, HD), BF16), rim, rim),
@@ -411,31 +412,32 @@
         (STATS, jax.ShapeDtypeStruct(HALF_SHAPE, F32), jax.ShapeDtypeStruct(HALF_SHAPE, BF16)),
         (query, grad_out, cap, stats),
     )
+    def rim_part(part, into, behind):
+        return call(
+            rim_grads_kernel, 2.2, [smem(), g, g, r, r, s], (r, r, t, t), (rim, rim, TURNS, TURNS),
+            (band_width, query, grad_out, west, east, stats), part, into, behind,
+        )
+
+    first = rim_part((0, 2), (), ())
     total = keep + swap(send, CMASK).astype(F32)
     total = total.reshape((4, 2) + total.shape[1:])
-    keep, send = total[:, 0], total[:, 1].astype(BF16)
+    keep, send = total[:, 0], after(total[:, 1].astype(BF16), first[0])
     received = swap(send, YMASK)
-    to_west, to_east, out_turned, query_turned = call(
-        rim_grads_kernel, 4.5, [smem(), g, g, r, r, s], (r, r, t, t),
-        (rim, rim, TURNS, TURNS),
-        (band_width, query, grad_out, west, east, stats), behind=(keep,),
-    )
+    to_west, to_east, out_turned, query_turned = rim_part((1, 2), first, (keep,))
     from_east = shift(to_west, -1)
     from_west = shift(to_east, 1)
 
     own_out = (grid, grid, jax.ShapeDtypeStruct((2,) + GRID, F32))
     own_in = (band_width, query, keys, values, grad_out, cap, stats, out_turned, query_turned)
 
-    def own_part(part, into):
-        kinds = [smem(), g, g, g, g, c, s, t, t]
-        return call(own_grads_kernel, 4, kinds, (g, g, w), own_out, own_in, part, into, (received,))
-
-    first = own_part((0, 2), ())
+    attended, query_grad, own = call(
+        own_grads_kernel, 8, [smem(), g, g, g, g, c, s, t, t], (g, g, w), own_out, own_in,
+        behind=(received,),
+    )
     total = keep + received.astype(F32)
     keep = total[:1]
     sends = total[1:].astype(BF16)
     caps = [swap(sends[n : n + 1], mask) for n, mask in enumerate(XMASKS)]
-    attended, query_grad, own = own_part((1, 2), first)
     v = pl.BlockSpec(memory_space=pltpu.VMEM)
     key_grad, value_grad = pl.pallas_call(
         join_kernel,

time: 51.8 us -> 51.9 us (level)
  the two profiles are of different devices: /device:TPU:8 before, /device:TPU:1 now
where the time goes in v3:
time: 51.9 us; the launch traced here: 51.8 us
  Pallas kernels  22.4 us (43%)
  starting transfers between devices  19.1 us (37%)
  waiting for transfers between devices  7.06 us (14%)
  local copies, waits for them, and re-layouts  2.23 us (4%)
  between operations  0.86 us (2%)
    pallas_call x6, Pallas kernels, call(): pl.pallas_call(whole, out_shape=out_shape, grid=(1,), in_specs=specs[:inp...  20 us
    ppermute x10, starting transfers between devices, swap(): return lax.ppermute(value, 'lon', [(i, i ^ mask) for i in range(LON)])  15.2 us
    ppermute x10, waiting for transfers between devices, swap(): return lax.ppermute(value, 'lon', [(i, i ^ mask) for i in range(LON)])  7.05 us
    ppermute x4, starting transfers between devices, shift(): lax.ppermute(value, 'lon', [(i, (i + steps) % LON) for i in range(LON)])  3.88 us
    unnamed x15, local copies, waits for them, and re-layouts  2.16 us
    pallas_call x1, Pallas kernels, shards(): pl.pallas_call(join_kernel, out_shape=(grid, grid), in_specs=[smem()] + [...  1.65 us
  transfers between devices with their start and end apart: 14, of which 4 were waited for; matrix products, arithmetic and copies ran while one was open for 0% of the time, Pallas kernels for 29%

profile of v3, /device:TPU:1, one launch (start us, length us, event | category | flops | bytes accessed | tf_op | source)
XLA Modules:
  0.0 51.8 jit_solution(8993387762040309272)
XLA Ops:
  0.6 0.0 copy-start.2
  0.6 0.0 copy-start.3
  0.7 1.1 %copy.51.refs_0_ = bf16[8,48,512]{2,1,0:T(8,128)(2,1)S(1)} copy(bf16[8,48,512]{2,1,0:T(8,128)(2,1)} %param.7) | data formatting | bytes 786432
  1.7 0.0 copy-start.1
  1.7 1.0 %copy.52.refs_1_ = bf16[8,48,512]{2,1,0:T(8,128)(2,1)S(1)} copy(bf16[8,48,512]{2,1,0:T(8,128)(2,1)} %param.8) | data formatting | bytes 786432
  2.7 0.0 copy-done.2
  2.8 0.0 copy-done.3
  2.8 0.0 copy-start
  2.8 0.0 copy-done.1
  2.8 0.7 %shard_map.95 = (bf16[1,2,16,512]{3,2,1,0:T(8,128)(2,1)S(1)}, bf16[2,8,32,512]{3,2,1,0:T(8,128)(2,1)S(1)}, bf16[2,8,32,512]{3,2,1,0:T(8,128)(2,1)S(1)}) custom-call(s32[16]{0:T(128)S(1)} %copy-done.1, bf16[8,48,512]{2,1,0:T(8,128)(2,1)S(1)} %get-tuple-element.28.k_ref.refs_2_, bf16[8,48,512]{2,1,0:T(8,128)(2,1)S(1)} %get-tuple-element.29.v_ref.refs_3_), custom_call_target="tpu_custom_call" | custom-call | bytes 3500000 | tf_op jit(solution)/shard_map/pallas_call | solution.py:382
  3.6 2.2 %collective-permute-start = (bf16[1,2,16,512]{3,2,1,0:T(8,128)(2,1)S(1)}, bf16[1,2,16,512]{3,2,1,0:T(8,128)(2,1)S(1)}, u32[]{:S(2)}, u32[]{:S(2)}) collective-permute-start(bf16[1,2,16,512]{3,2,1,0:T(8,128)(2,1)S(1)} %get-tuple-element.31), channel_id=1, source_target_pairs={{0,128},{16,144},{32,160},{48,176},{64,192},{80,208},{96,224},{112... | collective-permute-start | bytes 98312 | tf_op jit(solution)/shard_map/ppermute | solution.py:32
  5.8 2.1 %collective-permute-start.4 = (bf16[2,8,32,512]{3,2,1,0:T(8,128)(2,1)S(1)}, bf16[2,8,32,512]{3,2,1,0:T(8,128)(2,1)S(1)}, u32[]{:S(2)}, u32[]{:S(2)}) collective-permute-start(bf16[2,8,32,512]{3,2,1,0:T(8,128)(2,1)S(1)} %get-tuple-element.32), channel_id=1, source_target_pairs={{0,16},{16,32},{32,48},{48,64},{64,80},{80,96},{96,112},{112,128},... | collective-permute-start | bytes 1572872 | tf_op jit(solution)/shard_map/ppermute | solution.py:36
  7.9 0.0 collective-permute-start.5
  7.9 0.0 collective-permute-done.refs_5_
  7.9 1.3 %collective-permute-start.1 = (bf16[2,2,16,512]{3,2,1,0:T(8,128)(2,1)S(1)}, bf16[2,2,16,512]{3,2,1,0:T(8,128)(2,1)S(1)}, u32[]{:S(2)}, u32[]{:S(2)}) collective-permute-start(bf16[2,2,16,512]{3,2,1,0:T(8,128)(2,1)S(1)} %get-tuple-element.55), channel_id=1, source_target_pairs={{0,32},{16,48},{32,0},{48,16},{64,96},{80,112},{96,64},{112,80},{1... | collective-permute-start | bytes 196616 | tf_op jit(solution)/shard_map/ppermute | solution.py:32
  9.2 3.1 %collective-permute-start.2 = (bf16[2,2,16,512]{3,2,1,0:T(8,128)(2,1)S(1)}, bf16[2,2,16,512]{3,2,1,0:T(8,128)(2,1)S(1)}, u32[]{:S(2)}, u32[]{:S(2)}) collective-permute-start(bf16[2,2,16,512]{3,2,1,0:T(8,128)(2,1)S(1)} %get-tuple-element.55), channel_id=1, source_target_pairs={{0,64},{16,80},{32,96},{48,112},{64,0},{80,16},{96,32},{112,48},{1... | collective-permute-start | bytes 196616 | tf_op jit(solution)/shard_map/ppermute | solution.py:32
  12.2 0.0 collective-permute-start.3
  12.3 0.0 copy-done
  12.3 2.5 %shard_map.96.refs_5_ = f32[4,16,256]{2,1,0:T(8,128)S(1)} custom-call(s32[8]{0:T(128)S(1)} %copy-done, bf16[8,48,512]{2,1,0:T(8,128)(2,1)S(1)} %get-tuple-element.27.refs_1_.refs_0_, bf16[8,48,512]{2,1,0:T(8,128)(2,1)S(1)} %get-tuple-element.28.k_ref.refs_2_, bf16[8,48,512]{2,1,0:T(8,128)(2,1)S(1)} %get-tuple-element.29.v_ref.refs_3_, ...), custom_call_target="tpu_custom_call" | custom-call | bytes 1750000 | tf_op jit(solution)/shard_map/pallas_call | solution.py:110
  14.7 1.3 %collective-permute-done.1 = bf16[2,2,16,512]{3,2,1,0:T(8,128)(2,1)S(1)} collective-permute-done((bf16[2,2,16,512]{3,2,1,0:T(8,128)(2,1)S(1)}, bf16[2,2,16,512]{3,2,1,0:T(8,128)(2,1)S(1)}, u32[]{:S(2)}, u32[]{:S(2)}) %collective-permute-start.1) | collective-permute-done | bytes 65568 | tf_op jit(solution)/shard_map/ppermute | solution.py:32
  16.1 3.7 %collective-permute-done.2 = bf16[2,2,16,512]{3,2,1,0:T(8,128)(2,1)S(1)} collective-permute-done((bf16[2,2,16,512]{3,2,1,0:T(8,128)(2,1)S(1)}, bf16[2,2,16,512]{3,2,1,0:T(8,128)(2,1)S(1)}, u32[]{:S(2)}, u32[]{:S(2)}) %collective-permute-start.2) | collective-permute-done | bytes 65568 | tf_op jit(solution)/shard_map/ppermute | solution.py:32
  19.8 0.5 %collective-permute-done.3 = bf16[2,2,16,512]{3,2,1,0:T(8,128)(2,1)S(1)} collective-permute-done((bf16[2,2,16,512]{3,2,1,0:T(8,128)(2,1)S(1)}, bf16[2,2,16,512]{3,2,1,0:T(8,128)(2,1)S(1)}, u32[]{:S(2)}, u32[]{:S(2)}) %collective-permute-start.3) | collective-permute-done | bytes 65568 | tf_op jit(solution)/shard_map/ppermute | solution.py:32
  20.3 0.0 collective-permute-done.4.refs_3_
  20.3 0.0 collective-permute-done.5.refs_4_
  20.3 1.9 %shard_map.97.refs_1_.refs_3_ = f32[4,16,256]{2,1,0:T(8,128)S(1)} custom-call(s32[8]{0:T(128)S(1)} %copy-done, bf16[8,48,512]{2,1,0:T(8,128)(2,1)S(1)} %get-tuple-element.27.refs_1_.refs_0_, bf16[8,48,512]{2,1,0:T(8,128)(2,1)S(1)} %get-tuple-element.30.refs_4_.refs_2_.refs_1_, bf16[2,8,32,512]{3,2,1,0:T(8,128)(2,1)S(1)} %collective-permute-done.4.refs_3_, ...), custom_call_target="tpu_custom_call" | custom-call | bytes 1750000 | tf_op jit(solution)/shard_map/pallas_call | solution.py:110
  22.2 0.1 collective-permute-start.6
  22.4 1.5 %collective-permute-done.6 = bf16[8,2,16,512]{3,2,1,0:T(8,128)(2,1)S(1)} collective-permute-done((bf16[8,2,16,512]{3,2,1,0:T(8,128)(2,1)S(1)}, bf16[8,2,16,512]{3,2,1,0:T(8,128)(2,1)S(1)}, u32[]{:S(2)}, u32[]{:S(2)}) %collective-permute-start.6) | collective-permute-done | bytes 262176 | tf_op jit(solution)/shard_map/ppermute | solution.py:32
  23.9 2.9 %shard_map.99 = (f32[4,16,256]{2,1,0:T(8,128)S(1)}, f32[8,2,16,512]{3,2,1,0:T(8,128)S(1)}, bf16[8,2,16,512]{3,2,1,0:T(8,128)(2,1)S(1)}) custom-call(bf16[8,48,512]{2,1,0:T(8,128)(2,1)S(1)} %get-tuple-element.27.refs_1_.refs_0_, bf16[8,48,512]{2,1,0:T(8,128)(2,1)S(1)} %get-tuple-element.30.refs_4_.refs_2_.refs_1_, ...), custom_call_target="tpu_custom_call" | custom-call | bytes 10500000 | tf_op jit(solution)/shard_map/pallas_call | solution.py:110
  26.8 0.4 collective-permute-start.7
  27.2 2.6 %shard_map.100 = (bf16[2,8,32,512]{3,2,1,0:T(8,128)(2,1)S(1)}, bf16[2,8,32,512]{3,2,1,0:T(8,128)(2,1)S(1)}, f32[4,3,128,128]{3,2,1,0:T(8,128)S(1)}, f32[4,3,128,128]{3,2,1,0:T(8,128)S(1)}) custom-call(s32[8]{0:T(128)S(1)} %copy-done, bf16[8,48,512]{2,1,0:T(8,128)(2,1)S(1)} %get-tuple-element.27.refs_1_.refs_0_, ...), custom_call_target="tpu_custom_call" | custom-call | bytes 7700000 | tf_op jit(solution)/shard_map/pallas_call | solution.py:110
  29.9 0.0 collective-permute-done.7
  29.9 0.1 convert_add_fusion
  30.0 1.3 %collective-permute-start.8 = (bf16[4,2,16,512]{3,2,1,0:T(8,128)(2,1)S(1)}, bf16[4,2,16,512]{3,2,1,0:T(8,128)(2,1)S(1)}, u32[]{:S(2)}, u32[]{:S(2)}) collective-permute-start(bf16[4,2,16,512]{3,2,1,0:T(8,128)(2,1)S(1)} %shard_map.102), channel_id=1, source_target_pairs={{0,128},{16,144},{32,160},{48,176},{64,192},{80,208},{96,224},{112... | collective-permute-start | bytes 393224 | tf_op jit(solution)/shard_map/ppermute | solution.py:32
  31.3 2.6 %shard_map.101 = (bf16[2,8,32,512]{3,2,1,0:T(8,128)(2,1)S(1)}, bf16[2,8,32,512]{3,2,1,0:T(8,128)(2,1)S(1)}, f32[4,3,128,128]{3,2,1,0:T(8,128)S(1)}, f32[4,3,128,128]{3,2,1,0:T(8,128)S(1)}) custom-call(s32[8]{0:T(128)S(1)} %copy-done, ...), custom_call_target="tpu_custom_call", output_to_operand_aliasing={{0}: (6, {}), {1}: (7, {}), {2}: (8, {}), {3}: (9, {})} | custom-call | bytes 7700000 | tf_op jit(solution)/shard_map/pallas_call | solution.py:110
  33.9 0.5 collective-permute-start.10
  34.4 1.3 %collective-permute-start.9 = (bf16[2,8,32,512]{3,2,1,0:T(8,128)(2,1)S(1)}, bf16[2,8,32,512]{3,2,1,0:T(8,128)(2,1)S(1)}, u32[]{:S(2)}, u32[]{:S(2)}) collective-permute-start(bf16[2,8,32,512]{3,2,1,0:T(8,128)(2,1)S(1)} %get-tuple-element.46), channel_id=1, source_target_pairs={{0,16},{16,32},{32,48},{48,64},{64,80},{80,96},{96,112},{112,128},... | collective-permute-start | bytes 1572872 | tf_op jit(solution)/shard_map/ppermute | solution.py:36
  35.8 0.0 collective-permute-done.8.refs_9_
  35.8 0.7 %collective-permute-start.11 = (bf16[1,2,16,512]{3,2,1,0:T(8,128)(2,1)S(1)}, bf16[1,2,16,512]{3,2,1,0:T(8,128)(2,1)S(1)}, u32[]{:S(2)}, u32[]{:S(2)}) collective-permute-start(bf16[1,2,16,512]{3,2,1,0:T(8,128)(2,1)S(1)} %get-tuple-element.54), channel_id=1, source_target_pairs={{0,32},{16,48},{32,0},{48,16},{64,96},{80,112},{96,64},{112,80},{1... | collective-permute-start | bytes 98312 | tf_op jit(solution)/shard_map/ppermute | solution.py:32
  36.5 6.1 %collective-permute-start.12 = (bf16[1,2,16,512]{3,2,1,0:T(8,128)(2,1)S(1)}, bf16[1,2,16,512]{3,2,1,0:T(8,128)(2,1)S(1)}, u32[]{:S(2)}, u32[]{:S(2)}) collective-permute-start(bf16[1,2,16,512]{3,2,1,0:T(8,128)(2,1)S(1)} %get-tuple-element.53), channel_id=1, source_target_pairs={{0,64},{16,80},{32,96},{48,112},{64,0},{80,16},{96,32},{112,48},{1... | collective-permute-start | bytes 98312 | tf_op jit(solution)/shard_map/ppermute | solution.py:32
  42.6 0.0 collective-permute-start.13
  42.6 7.5 %shard_map.103 = (bf16[8,48,512]{2,1,0:T(8,128)(2,1)}, bf16[8,48,512]{2,1,0:T(8,128)(2,1)}, f32[2,8,48,512]{3,2,1,0:T(8,128)S(1)}) custom-call(s32[8]{0:T(128)S(1)} %copy-done, bf16[8,48,512]{2,1,0:T(8,128)(2,1)S(1)} %get-tuple-element.27.refs_1_.refs_0_, bf16[8,48,512]{2,1,0:T(8,128)(2,1)S(1)} %get-tuple-element.28.k_ref.refs_2_, ...), custom_call_target="tpu_custom_call" | custom-call | bytes 28000000 | tf_op jit(solution)/shard_map/pallas_call | solution.py:110
  50.1 0.0 collective-permute-done.11.refs_0_
  50.1 0.0 collective-permute-done.12.refs_1_
  50.1 0.0 collective-permute-done.13.refs_2_
  50.1 0.0 collective-permute-done.10.east_ref
  50.1 0.0 collective-permute-done.9.west_ref
  50.1 1.6 %shard_map.104 = (bf16[8,48,512]{2,1,0:T(8,128)(2,1)}, bf16[8,48,512]{2,1,0:T(8,128)(2,1)}) custom-call(s32[16]{0:T(128)S(1)} %copy-done.1, f32[2,8,48,512]{3,2,1,0:T(8,128)S(1)} %get-tuple-element.45.own_ref, bf16[2,8,32,512]{3,2,1,0:T(8,128)(2,1)S(1)} %collective-permute-done.9.west_ref, bf16[2,8,32,512]{3,2,1,0:T(8,128)(2,1)S(1)} %collective-permute-done.10.east_ref, ...), custom_call_target="tpu_custom_call" | custom-call | bytes 7000000 | tf_op jit(solution)/shard_map/pallas_call | solution.py:442
  (17 shorter events, 0.2 us)
Async XLA Ops:
  0.6 2.1 %copy-start.2 = (bf16[8,48,512]{2,1,0:T(8,128)(2,1)S(1)}, bf16[8,48,512]{2,1,0:T(8,128)(2,1)}, u32[]{:S(2)}) copy-start(bf16[8,48,512]{2,1,0:T(8,128)(2,1)} %param.6) | copy-start | bytes 1179652
  0.6 2.1 %copy-start.3 = (bf16[8,48,512]{2,1,0:T(8,128)(2,1)S(1)}, bf16[8,48,512]{2,1,0:T(8,128)(2,1)}, u32[]{:S(2)}) copy-start(bf16[8,48,512]{2,1,0:T(8,128)(2,1)} %param.9) | copy-start | bytes 1179652
  1.7 1.1 %copy-start.1 = (s32[16]{0:T(128)S(1)}, s32[16]{0:T(128)}, u32[]{:S(2)}) copy-start(s32[16]{0:T(128)} %cap_blocks_ref.3) | copy-start | bytes 196
  2.8 9.5 %copy-start = (s32[8]{0:T(128)S(1)}, s32[8]{0:T(128)}, u32[]{:S(2)}) copy-start(s32[8]{0:T(128)} %refs_0_.11) | copy-start | bytes 100
  3.6 4.3 %collective-permute-start = (bf16[1,2,16,512]{3,2,1,0:T(8,128)(2,1)S(1)}, bf16[1,2,16,512]{3,2,1,0:T(8,128)(2,1)S(1)}, u32[]{:S(2)}, u32[]{:S(2)}) collective-permute-start(bf16[1,2,16,512]{3,2,1,0:T(8,128)(2,1)S(1)} %get-tuple-element.31), channel_id=1, source_target_pairs={{0,128},{16,144},{32,160},{48,176},{64,192},{80,208},{96,224},{112... | collective-permute-start | bytes 98312 | tf_op jit(solution)/shard_map/ppermute | solution.py:32
  5.8 14.5 %collective-permute-start.4 = (bf16[2,8,32,512]{3,2,1,0:T(8,128)(2,1)S(1)}, bf16[2,8,32,512]{3,2,1,0:T(8,128)(2,1)S(1)}, u32[]{:S(2)}, u32[]{:S(2)}) collective-permute-start(bf16[2,8,32,512]{3,2,1,0:T(8,128)(2,1)S(1)} %get-tuple-element.32), channel_id=1, source_target_pairs={{0,16},{16,32},{32,48},{48,64},{64,80},{80,96},{96,112},{112,128},... | collective-permute-start | bytes 1572872 | tf_op jit(solution)/shard_map/ppermute | solution.py:36
  7.9 12.5 %collective-permute-start.5 = (bf16[2,8,32,512]{3,2,1,0:T(8,128)(2,1)S(1)}, bf16[2,8,32,512]{3,2,1,0:T(8,128)(2,1)S(1)}, u32[]{:S(2)}, u32[]{:S(2)}) collective-permute-start(bf16[2,8,32,512]{3,2,1,0:T(8,128)(2,1)S(1)} %get-tuple-element.33), channel_id=1, source_target_pairs={{0,240},{16,0},{32,16},{48,32},{64,48},{80,64},{96,80},{112,96},{1... | collective-permute-start | bytes 1572872 | tf_op jit(solution)/shard_map/ppermute | solution.py:36
  7.9 8.2 %collective-permute-start.1 = (bf16[2,2,16,512]{3,2,1,0:T(8,128)(2,1)S(1)}, bf16[2,2,16,512]{3,2,1,0:T(8,128)(2,1)S(1)}, u32[]{:S(2)}, u32[]{:S(2)}) collective-permute-start(bf16[2,2,16,512]{3,2,1,0:T(8,128)(2,1)S(1)} %get-tuple-element.55), channel_id=1, source_target_pairs={{0,32},{16,48},{32,0},{48,16},{64,96},{80,112},{96,64},{112,80},{1... | collective-permute-start | bytes 196616 | tf_op jit(solution)/shard_map/ppermute | solution.py:32
  9.2 10.6 %collective-permute-start.2 = (bf16[2,2,16,512]{3,2,1,0:T(8,128)(2,1)S(1)}, bf16[2,2,16,512]{3,2,1,0:T(8,128)(2,1)S(1)}, u32[]{:S(2)}, u32[]{:S(2)}) collective-permute-start(bf16[2,2,16,512]{3,2,1,0:T(8,128)(2,1)S(1)} %get-tuple-element.55), channel_id=1, source_target_pairs={{0,64},{16,80},{32,96},{48,112},{64,0},{80,16},{96,32},{112,48},{1... | collective-permute-start | bytes 196616 | tf_op jit(solution)/shard_map/ppermute | solution.py:32
  12.2 8.1 %collective-permute-start.3 = (bf16[2,2,16,512]{3,2,1,0:T(8,128)(2,1)S(1)}, bf16[2,2,16,512]{3,2,1,0:T(8,128)(2,1)S(1)}, u32[]{:S(2)}, u32[]{:S(2)}) collective-permute-start(bf16[2,2,16,512]{3,2,1,0:T(8,128)(2,1)S(1)} %get-tuple-element.55), channel_id=1, source_target_pairs={{0,96},{16,112},{32,64},{48,80},{64,32},{80,48},{96,0},{112,16},{1... | collective-permute-start | bytes 196616 | tf_op jit(solution)/shard_map/ppermute | solution.py:32
  22.2 1.6 %collective-permute-start.6 = (bf16[8,2,16,512]{3,2,1,0:T(8,128)(2,1)S(1)}, bf16[8,2,16,512]{3,2,1,0:T(8,128)(2,1)S(1)}, u32[]{:S(2)}, u32[]{:S(2)}) collective-permute-start(bf16[8,2,16,512]{3,2,1,0:T(8,128)(2,1)S(1)} %shard_map.98), channel_id=1, source_target_pairs={{0,16},{16,0},{32,48},{48,32},{64,80},{80,64},{96,112},{112,96},{1... | collective-permute-start | bytes 786440 | tf_op jit(solution)/shard_map/ppermute | solution.py:32
  26.8 3.0 %collective-permute-start.7 = (bf16[8,2,16,512]{3,2,1,0:T(8,128)(2,1)S(1)}, bf16[8,2,16,512]{3,2,1,0:T(8,128)(2,1)S(1)}, u32[]{:S(2)}, u32[]{:S(2)}) collective-permute-start(bf16[8,2,16,512]{3,2,1,0:T(8,128)(2,1)S(1)} %get-tuple-element.40), channel_id=1, source_target_pairs={{0,16},{16,0},{32,48},{48,32},{64,80},{80,64},{96,112},{112,96},{1... | collective-permute-start | bytes 786440 | tf_op jit(solution)/shard_map/ppermute | solution.py:32
  30.0 5.8 %collective-permute-start.8 = (bf16[4,2,16,512]{3,2,1,0:T(8,128)(2,1)S(1)}, bf16[4,2,16,512]{3,2,1,0:T(8,128)(2,1)S(1)}, u32[]{:S(2)}, u32[]{:S(2)}) collective-permute-start(bf16[4,2,16,512]{3,2,1,0:T(8,128)(2,1)S(1)} %shard_map.102), channel_id=1, source_target_pairs={{0,128},{16,144},{32,160},{48,176},{64,192},{80,208},{96,224},{112... | collective-permute-start | bytes 393224 | tf_op jit(solution)/shard_map/ppermute | solution.py:32
  33.9 16.2 %collective-permute-start.10 = (bf16[2,8,32,512]{3,2,1,0:T(8,128)(2,1)S(1)}, bf16[2,8,32,512]{3,2,1,0:T(8,128)(2,1)S(1)}, u32[]{:S(2)}, u32[]{:S(2)}) collective-permute-start(bf16[2,8,32,512]{3,2,1,0:T(8,128)(2,1)S(1)} %get-tuple-element.47), channel_id=1, source_target_pairs={{0,240},{16,0},{32,16},{48,32},{64,48},{80,64},{96,80},{112,96},{1... | collective-permute-start | bytes 1572872 | tf_op jit(solution)/shard_map/ppermute | solution.py:36
  34.4 15.7 %collective-permute-start.9 = (bf16[2,8,32,512]{3,2,1,0:T(8,128)(2,1)S(1)}, bf16[2,8,32,512]{3,2,1,0:T(8,128)(2,1)S(1)}, u32[]{:S(2)}, u32[]{:S(2)}) collective-permute-start(bf16[2,8,32,512]{3,2,1,0:T(8,128)(2,1)S(1)} %get-tuple-element.46), channel_id=1, source_target_pairs={{0,16},{16,32},{32,48},{48,64},{64,80},{80,96},{96,112},{112,128},... | collective-permute-start | bytes 1572872 | tf_op jit(solution)/shard_map/ppermute | solution.py:36
  35.8 14.3 %collective-permute-start.11 = (bf16[1,2,16,512]{3,2,1,0:T(8,128)(2,1)S(1)}, bf16[1,2,16,512]{3,2,1,0:T(8,128)(2,1)S(1)}, u32[]{:S(2)}, u32[]{:S(2)}) collective-permute-start(bf16[1,2,16,512]{3,2,1,0:T(8,128)(2,1)S(1)} %get-tuple-element.54), channel_id=1, source_target_pairs={{0,32},{16,48},{32,0},{48,16},{64,96},{80,112},{96,64},{112,80},{1... | collective-permute-start | bytes 98312 | tf_op jit(solution)/shard_map/ppermute | solution.py:32
  36.5 13.6 %collective-permute-start.12 = (bf16[1,2,16,512]{3,2,1,0:T(8,128)(2,1)S(1)}, bf16[1,2,16,512]{3,2,1,0:T(8,128)(2,1)S(1)}, u32[]{:S(2)}, u32[]{:S(2)}) collective-permute-start(bf16[1,2,16,512]{3,2,1,0:T(8,128)(2,1)S(1)} %get-tuple-element.53), channel_id=1, source_target_pairs={{0,64},{16,80},{32,96},{48,112},{64,0},{80,16},{96,32},{112,48},{1... | collective-permute-start | bytes 98312 | tf_op jit(solution)/shard_map/ppermute | solution.py:32
  42.6 7.5 %collective-permute-start.13 = (bf16[1,2,16,512]{3,2,1,0:T(8,128)(2,1)S(1)}, bf16[1,2,16,512]{3,2,1,0:T(8,128)(2,1)S(1)}, u32[]{:S(2)}, u32[]{:S(2)}) collective-permute-start(bf16[1,2,16,512]{3,2,1,0:T(8,128)(2,1)S(1)} %get-tuple-element.52), channel_id=1, source_target_pairs={{0,96},{16,112},{32,64},{48,80},{64,32},{80,48},{96,0},{112,16},{1... | collective-permute-start | bytes 98312 | tf_op jit(solution)/shard_map/ppermute | solution.py:32

commit v4 on v3

--- a/solution.py
+++ b/solution.py
@@ -430,14 +430,16 @@
     own_out = (grid, grid, jax.ShapeDtypeStruct((2,) + GRID, F32))
     own_in = (band_width, query, keys, values, grad_out, cap, stats, out_turned, query_turned)
 
-    attended, query_grad, own = call(
-        own_grads_kernel, 8, [smem(), g, g, g, g, c, s, t, t], (g, g, w), own_out, own_in,
-        behind=(received,),
-    )
+    def own_part(part, into):
+        kinds = [smem(), g, g, g, g, c, s, t, t]
+        return call(own_grads_kernel, 4, kinds, (g, g, w), own_out, own_in, part, into, (received,))
+
+    first = own_part((0, 2), ())
     total = keep + received.astype(F32)
     keep = total[:1]
-    sends = total[1:].astype(BF16)
+    sends = after(total[1:].astype(BF16), first[2])
     caps = [swap(sends[n : n + 1], mask) for n, mask in enumerate(XMASKS)]
+    attended, query_grad, own = own_part((1, 2), first)
     v = pl.BlockSpec(memory_space=pltpu.VMEM)
     key_grad, value_grad = pl.pallas_call(
         join_kernel,

time: 51.9 us -> 50.9 us (0.981)
  the two profiles are of different devices: /device:TPU:1 before, /device:TPU:8 now
where the time goes in v4:
time: 50.9 us; the launch traced here: 50.8 us
  Pallas kernels  23.8 us (47%)
  starting transfers between devices  20.1 us (39%)
  waiting for transfers between devices  3.63 us (7%)
  local copies, waits for them, and re-layouts  2.24 us (4%)
  between operations  0.88 us (2%)
    pallas_call x7, Pallas kernels, call(): pl.pallas_call(whole, out_shape=out_shape, grid=(1,), in_specs=specs[:inp...  21.4 us
    ppermute x10, starting transfers between devices, swap(): return lax.ppermute(value, 'lon', [(i, i ^ mask) for i in range(LON)])  12.3 us
    ppermute x4, starting transfers between devices, shift(): lax.ppermute(value, 'lon', [(i, (i + steps) % LON) for i in range(LON)])  7.78 us
    ppermute x10, waiting for transfers between devices, swap(): return lax.ppermute(value, 'lon', [(i, i ^ mask) for i in range(LON)])  3.62 us
    unnamed x15, local copies, waits for them, and re-layouts  2.16 us
    pallas_call x1, Pallas kernels, shards(): pl.pallas_call(join_kernel, out_shape=(grid, grid), in_specs=[smem()] + [...  1.65 us
  transfers between devices with their start and end apart: 14, of which 4 were waited for; matrix products, arithmetic and copies ran while one was open for 0% of the time, Pallas kernels for 33%

profile of v4, /device:TPU:8, one launch (start us, length us, event | category | flops | bytes accessed | tf_op | source)
XLA Modules:
  0.0 50.8 jit_solution(14358243937704337779)
XLA Ops:
  0.6 0.0 copy-start.2
  0.6 0.0 copy-start.3
  0.7 1.1 %copy.58.refs_0_ = bf16[8,48,512]{2,1,0:T(8,128)(2,1)S(1)} copy(bf16[8,48,512]{2,1,0:T(8,128)(2,1)} %param.7) | data formatting | bytes 786432
  1.7 0.0 copy-start.1
  1.7 1.0 %copy.59.refs_1_ = bf16[8,48,512]{2,1,0:T(8,128)(2,1)S(1)} copy(bf16[8,48,512]{2,1,0:T(8,128)(2,1)} %param.8) | data formatting | bytes 786432
  2.7 0.0 copy-done.2
  2.8 0.0 copy-done.3
  2.8 0.0 copy-start
  2.8 0.0 copy-done.1
  2.8 0.7 %shard_map.95 = (bf16[1,2,16,512]{3,2,1,0:T(8,128)(2,1)S(1)}, bf16[2,8,32,512]{3,2,1,0:T(8,128)(2,1)S(1)}, bf16[2,8,32,512]{3,2,1,0:T(8,128)(2,1)S(1)}) custom-call(s32[16]{0:T(128)S(1)} %copy-done.1, bf16[8,48,512]{2,1,0:T(8,128)(2,1)S(1)} %get-tuple-element.31.k_ref.refs_2_, bf16[8,48,512]{2,1,0:T(8,128)(2,1)S(1)} %get-tuple-element.32.v_ref.refs_3_), custom_call_target="tpu_custom_call" | custom-call | bytes 3500000 | tf_op jit(solution)/shard_map/pallas_call | solution.py:382
  3.6 2.3 %collective-permute-start = (bf16[1,2,16,512]{3,2,1,0:T(8,128)(2,1)S(1)}, bf16[1,2,16,512]{3,2,1,0:T(8,128)(2,1)S(1)}, u32[]{:S(2)}, u32[]{:S(2)}) collective-permute-start(bf16[1,2,16,512]{3,2,1,0:T(8,128)(2,1)S(1)} %get-tuple-element.34), channel_id=1, source_target_pairs={{0,128},{16,144},{32,160},{48,176},{64,192},{80,208},{96,224},{112... | collective-permute-start | bytes 98312 | tf_op jit(solution)/shard_map/ppermute | solution.py:32
  5.9 0.0 collective-permute-start.4
  5.9 3.9 %collective-permute-start.5 = (bf16[2,8,32,512]{3,2,1,0:T(8,128)(2,1)S(1)}, bf16[2,8,32,512]{3,2,1,0:T(8,128)(2,1)S(1)}, u32[]{:S(2)}, u32[]{:S(2)}) collective-permute-start(bf16[2,8,32,512]{3,2,1,0:T(8,128)(2,1)S(1)} %get-tuple-element.36), channel_id=1, source_target_pairs={{0,240},{16,0},{32,16},{48,32},{64,48},{80,64},{96,80},{112,96},{1... | collective-permute-start | bytes 1572872 | tf_op jit(solution)/shard_map/ppermute | solution.py:36
  9.7 0.0 collective-permute-done.refs_5_
  9.7 0.1 collective-permute-start.1
  9.9 1.3 %collective-permute-start.3 = (bf16[2,2,16,512]{3,2,1,0:T(8,128)(2,1)S(1)}, bf16[2,2,16,512]{3,2,1,0:T(8,128)(2,1)S(1)}, u32[]{:S(2)}, u32[]{:S(2)}) collective-permute-start(bf16[2,2,16,512]{3,2,1,0:T(8,128)(2,1)S(1)} %get-tuple-element.59), channel_id=1, source_target_pairs={{0,96},{16,112},{32,64},{48,80},{64,32},{80,48},{96,0},{112,16},{1... | collective-permute-start | bytes 196616 | tf_op jit(solution)/shard_map/ppermute | solution.py:32
  11.2 2.7 %collective-permute-start.2 = (bf16[2,2,16,512]{3,2,1,0:T(8,128)(2,1)S(1)}, bf16[2,2,16,512]{3,2,1,0:T(8,128)(2,1)S(1)}, u32[]{:S(2)}, u32[]{:S(2)}) collective-permute-start(bf16[2,2,16,512]{3,2,1,0:T(8,128)(2,1)S(1)} %get-tuple-element.59), channel_id=1, source_target_pairs={{0,64},{16,80},{32,96},{48,112},{64,0},{80,16},{96,32},{112,48},{1... | collective-permute-start | bytes 196616 | tf_op jit(solution)/shard_map/ppermute | solution.py:32
  13.9 0.0 copy-done
  13.9 2.5 %shard_map.96.refs_5_ = f32[4,16,256]{2,1,0:T(8,128)S(1)} custom-call(s32[8]{0:T(128)S(1)} %copy-done, bf16[8,48,512]{2,1,0:T(8,128)(2,1)S(1)} %get-tuple-element.30.refs_1_.refs_0_, bf16[8,48,512]{2,1,0:T(8,128)(2,1)S(1)} %get-tuple-element.31.k_ref.refs_2_, bf16[8,48,512]{2,1,0:T(8,128)(2,1)S(1)} %get-tuple-element.32.v_ref.refs_3_, ...), custom_call_target="tpu_custom_call" | custom-call | bytes 1750000 | tf_op jit(solution)/shard_map/pallas_call | solution.py:110
  16.4 0.2 collective-permute-done.1
  16.6 1.2 %collective-permute-done.2 = bf16[2,2,16,512]{3,2,1,0:T(8,128)(2,1)S(1)} collective-permute-done((bf16[2,2,16,512]{3,2,1,0:T(8,128)(2,1)S(1)}, bf16[2,2,16,512]{3,2,1,0:T(8,128)(2,1)S(1)}, u32[]{:S(2)}, u32[]{:S(2)}) %collective-permute-start.2) | collective-permute-done | bytes 65568 | tf_op jit(solution)/shard_map/ppermute | solution.py:32
  17.8 0.7 %collective-permute-done.3 = bf16[2,2,16,512]{3,2,1,0:T(8,128)(2,1)S(1)} collective-permute-done((bf16[2,2,16,512]{3,2,1,0:T(8,128)(2,1)S(1)}, bf16[2,2,16,512]{3,2,1,0:T(8,128)(2,1)S(1)}, u32[]{:S(2)}, u32[]{:S(2)}) %collective-permute-start.3) | collective-permute-done | bytes 65568 | tf_op jit(solution)/shard_map/ppermute | solution.py:32
  18.5 0.0 collective-permute-done.4.refs_3_
  18.5 0.0 collective-permute-done.5.refs_4_
  18.5 1.9 %shard_map.97.refs_1_.refs_3_ = f32[4,16,256]{2,1,0:T(8,128)S(1)} custom-call(s32[8]{0:T(128)S(1)} %copy-done, bf16[8,48,512]{2,1,0:T(8,128)(2,1)S(1)} %get-tuple-element.30.refs_1_.refs_0_, bf16[8,48,512]{2,1,0:T(8,128)(2,1)S(1)} %get-tuple-element.33.refs_4_.refs_2_.refs_1_, bf16[2,8,32,512]{3,2,1,0:T(8,128)(2,1)S(1)} %collective-permute-done.4.refs_3_, ...), custom_call_target="tpu_custom_call" | custom-call | bytes 1750000 | tf_op jit(solution)/shard_map/pallas_call | solution.py:110
  20.4 0.1 collective-permute-start.6
  20.5 1.5 %collective-permute-done.6 = bf16[8,2,16,512]{3,2,1,0:T(8,128)(2,1)S(1)} collective-permute-done((bf16[8,2,16,512]{3,2,1,0:T(8,128)(2,1)S(1)}, bf16[8,2,16,512]{3,2,1,0:T(8,128)(2,1)S(1)}, u32[]{:S(2)}, u32[]{:S(2)}) %collective-permute-start.6) | collective-permute-done | bytes 262176 | tf_op jit(solution)/shard_map/ppermute | solution.py:32
  22.1 2.9 %shard_map.99 = (f32[4,16,256]{2,1,0:T(8,128)S(1)}, f32[8,2,16,512]{3,2,1,0:T(8,128)S(1)}, bf16[8,2,16,512]{3,2,1,0:T(8,128)(2,1)S(1)}) custom-call(bf16[8,48,512]{2,1,0:T(8,128)(2,1)S(1)} %get-tuple-element.30.refs_1_.refs_0_, bf16[8,48,512]{2,1,0:T(8,128)(2,1)S(1)} %get-tuple-element.33.refs_4_.refs_2_.refs_1_, ...), custom_call_target="tpu_custom_call" | custom-call | bytes 10500000 | tf_op jit(solution)/shard_map/pallas_call | solution.py:110
  25.0 0.4 collective-permute-start.7
  25.4 2.6 %shard_map.100 = (bf16[2,8,32,512]{3,2,1,0:T(8,128)(2,1)S(1)}, bf16[2,8,32,512]{3,2,1,0:T(8,128)(2,1)S(1)}, f32[4,3,128,128]{3,2,1,0:T(8,128)S(1)}, f32[4,3,128,128]{3,2,1,0:T(8,128)S(1)}) custom-call(s32[8]{0:T(128)S(1)} %copy-done, bf16[8,48,512]{2,1,0:T(8,128)(2,1)S(1)} %get-tuple-element.30.refs_1_.refs_0_, ...), custom_call_target="tpu_custom_call" | custom-call | bytes 7700000 | tf_op jit(solution)/shard_map/pallas_call | solution.py:110
  28.1 0.0 collective-permute-done.7
  28.1 0.1 convert_add_fusion
  28.2 1.2 %collective-permute-start.8 = (bf16[4,2,16,512]{3,2,1,0:T(8,128)(2,1)S(1)}, bf16[4,2,16,512]{3,2,1,0:T(8,128)(2,1)S(1)}, u32[]{:S(2)}, u32[]{:S(2)}) collective-permute-start(bf16[4,2,16,512]{3,2,1,0:T(8,128)(2,1)S(1)} %shard_map.102), channel_id=1, source_target_pairs={{0,128},{16,144},{32,160},{48,176},{64,192},{80,208},{96,224},{112... | collective-permute-start | bytes 393224 | tf_op jit(solution)/shard_map/ppermute | solution.py:32
  29.4 2.6 %shard_map.101 = (bf16[2,8,32,512]{3,2,1,0:T(8,128)(2,1)S(1)}, bf16[2,8,32,512]{3,2,1,0:T(8,128)(2,1)S(1)}, f32[4,3,128,128]{3,2,1,0:T(8,128)S(1)}, f32[4,3,128,128]{3,2,1,0:T(8,128)S(1)}) custom-call(s32[8]{0:T(128)S(1)} %copy-done, ...), custom_call_target="tpu_custom_call", output_to_operand_aliasing={{0}: (6, {}), {1}: (7, {}), {2}: (8, {}), {3}: (9, {})} | custom-call | bytes 7700000 | tf_op jit(solution)/shard_map/pallas_call | solution.py:110
  32.1 0.1 collective-permute-start.9
  32.2 3.8 %collective-permute-start.10 = (bf16[2,8,32,512]{3,2,1,0:T(8,128)(2,1)S(1)}, bf16[2,8,32,512]{3,2,1,0:T(8,128)(2,1)S(1)}, u32[]{:S(2)}, u32[]{:S(2)}) collective-permute-start(bf16[2,8,32,512]{3,2,1,0:T(8,128)(2,1)S(1)} %get-tuple-element.53), channel_id=1, source_target_pairs={{0,240},{16,0},{32,16},{48,32},{64,48},{80,64},{96,80},{112,96},{1... | collective-permute-start | bytes 1572872 | tf_op jit(solution)/shard_map/ppermute | solution.py:36
  36.0 0.0 collective-permute-done.8.refs_9_.refs_12_
  36.1 4.4 %shard_map.103 = (bf16[8,48,512]{2,1,0:T(8,128)(2,1)}, bf16[8,48,512]{2,1,0:T(8,128)(2,1)}, f32[2,8,48,512]{3,2,1,0:T(8,128)S(1)}) custom-call(s32[8]{0:T(128)S(1)} %copy-done, bf16[8,48,512]{2,1,0:T(8,128)(2,1)S(1)} %get-tuple-element.30.refs_1_.refs_0_, bf16[8,48,512]{2,1,0:T(8,128)(2,1)S(1)} %get-tuple-element.31.k_ref.refs_2_, ...), custom_call_target="tpu_custom_call" | custom-call | bytes 14000000 | tf_op jit(solution)/shard_map/pallas_call | solution.py:110
  40.5 1.8 %collective-permute-start.13 = (bf16[1,2,16,512]{3,2,1,0:T(8,128)(2,1)S(1)}, bf16[1,2,16,512]{3,2,1,0:T(8,128)(2,1)S(1)}, u32[]{:S(2)}, u32[]{:S(2)}) collective-permute-start(bf16[1,2,16,512]{3,2,1,0:T(8,128)(2,1)S(1)} %get-tuple-element.56), channel_id=1, source_target_pairs={{0,96},{16,112},{32,64},{48,80},{64,32},{80,48},{96,0},{112,16},{1... | collective-permute-start | bytes 98312 | tf_op jit(solution)/shard_map/ppermute | solution.py:32
  42.3 0.0 collective-permute-start.12
  42.3 2.3 %collective-permute-start.11 = (bf16[1,2,16,512]{3,2,1,0:T(8,128)(2,1)S(1)}, bf16[1,2,16,512]{3,2,1,0:T(8,128)(2,1)S(1)}, u32[]{:S(2)}, u32[]{:S(2)}) collective-permute-start(bf16[1,2,16,512]{3,2,1,0:T(8,128)(2,1)S(1)} %get-tuple-element.58), channel_id=1, source_target_pairs={{0,32},{16,48},{32,0},{48,16},{64,96},{80,112},{96,64},{112,80},{1... | collective-permute-start | bytes 98312 | tf_op jit(solution)/shard_map/ppermute | solution.py:32
  44.7 4.4 %shard_map.104 = (bf16[8,48,512]{2,1,0:T(8,128)(2,1)}, bf16[8,48,512]{2,1,0:T(8,128)(2,1)}, f32[2,8,48,512]{3,2,1,0:T(8,128)S(1)}) custom-call(s32[8]{0:T(128)S(1)} %copy-done, bf16[8,48,512]{2,1,0:T(8,128)(2,1)S(1)} %get-tuple-element.30.refs_1_.refs_0_, ...), custom_call_target="tpu_custom_call", output_to_operand_aliasing={{0}: (9, {}), {1}: (10, {}), {2}: (11, {})} | custom-call | bytes 14000000 | tf_op jit(solution)/shard_map/pallas_call | solution.py:110
  49.1 0.0 collective-permute-done.13.refs_2_
  49.1 0.0 collective-permute-done.12.refs_1_
  49.1 0.0 collective-permute-done.11.refs_0_
  49.1 0.0 collective-permute-done.9.west_ref
  49.1 0.0 collective-permute-done.10.east_ref
  49.1 1.6 %shard_map.106 = (bf16[8,48,512]{2,1,0:T(8,128)(2,1)}, bf16[8,48,512]{2,1,0:T(8,128)(2,1)}) custom-call(s32[16]{0:T(128)S(1)} %copy-done.1, f32[2,8,48,512]{3,2,1,0:T(8,128)S(1)} %get-tuple-element.51.own_ref, bf16[2,8,32,512]{3,2,1,0:T(8,128)(2,1)S(1)} %collective-permute-done.9.west_ref, bf16[2,8,32,512]{3,2,1,0:T(8,128)(2,1)S(1)} %collective-permute-done.10.east_ref, ...), custom_call_target="tpu_custom_call" | custom-call | bytes 7000000 | tf_op jit(solution)/shard_map/pallas_call | solution.py:444
  (19 shorter events, 0.2 us)
Async XLA Ops:
  0.6 2.1 %copy-start.2 = (bf16[8,48,512]{2,1,0:T(8,128)(2,1)S(1)}, bf16[8,48,512]{2,1,0:T(8,128)(2,1)}, u32[]{:S(2)}) copy-start(bf16[8,48,512]{2,1,0:T(8,128)(2,1)} %param.6) | copy-start | bytes 1179652
  0.6 2.1 %copy-start.3 = (bf16[8,48,512]{2,1,0:T(8,128)(2,1)S(1)}, bf16[8,48,512]{2,1,0:T(8,128)(2,1)}, u32[]{:S(2)}) copy-start(bf16[8,48,512]{2,1,0:T(8,128)(2,1)} %param.9) | copy-start | bytes 1179652
  1.7 1.1 %copy-start.1 = (s32[16]{0:T(128)S(1)}, s32[16]{0:T(128)}, u32[]{:S(2)}) copy-start(s32[16]{0:T(128)} %cap_blocks_ref.3) | copy-start | bytes 196
  2.8 11.2 %copy-start = (s32[8]{0:T(128)S(1)}, s32[8]{0:T(128)}, u32[]{:S(2)}) copy-start(s32[8]{0:T(128)} %refs_0_.13) | copy-start | bytes 100
  3.6 6.1 %collective-permute-start = (bf16[1,2,16,512]{3,2,1,0:T(8,128)(2,1)S(1)}, bf16[1,2,16,512]{3,2,1,0:T(8,128)(2,1)S(1)}, u32[]{:S(2)}, u32[]{:S(2)}) collective-permute-start(bf16[1,2,16,512]{3,2,1,0:T(8,128)(2,1)S(1)} %get-tuple-element.34), channel_id=1, source_target_pairs={{0,128},{16,144},{32,160},{48,176},{64,192},{80,208},{96,224},{112... | collective-permute-start | bytes 98312 | tf_op jit(solution)/shard_map/ppermute | solution.py:32
  5.9 12.7 %collective-permute-start.4 = (bf16[2,8,32,512]{3,2,1,0:T(8,128)(2,1)S(1)}, bf16[2,8,32,512]{3,2,1,0:T(8,128)(2,1)S(1)}, u32[]{:S(2)}, u32[]{:S(2)}) collective-permute-start(bf16[2,8,32,512]{3,2,1,0:T(8,128)(2,1)S(1)} %get-tuple-element.35), channel_id=1, source_target_pairs={{0,16},{16,32},{32,48},{48,64},{64,80},{80,96},{96,112},{112,128},... | collective-permute-start | bytes 1572872 | tf_op jit(solution)/shard_map/ppermute | solution.py:36
  5.9 12.7 %collective-permute-start.5 = (bf16[2,8,32,512]{3,2,1,0:T(8,128)(2,1)S(1)}, bf16[2,8,32,512]{3,2,1,0:T(8,128)(2,1)S(1)}, u32[]{:S(2)}, u32[]{:S(2)}) collective-permute-start(bf16[2,8,32,512]{3,2,1,0:T(8,128)(2,1)S(1)} %get-tuple-element.36), channel_id=1, source_target_pairs={{0,240},{16,0},{32,16},{48,32},{64,48},{80,64},{96,80},{112,96},{1... | collective-permute-start | bytes 1572872 | tf_op jit(solution)/shard_map/ppermute | solution.py:36
  9.7 6.9 %collective-permute-start.1 = (bf16[2,2,16,512]{3,2,1,0:T(8,128)(2,1)S(1)}, bf16[2,2,16,512]{3,2,1,0:T(8,128)(2,1)S(1)}, u32[]{:S(2)}, u32[]{:S(2)}) collective-permute-start(bf16[2,2,16,512]{3,2,1,0:T(8,128)(2,1)S(1)} %get-tuple-element.59), channel_id=1, source_target_pairs={{0,32},{16,48},{32,0},{48,16},{64,96},{80,112},{96,64},{112,80},{1... | collective-permute-start | bytes 196616 | tf_op jit(solution)/shard_map/ppermute | solution.py:32
  9.9 8.7 %collective-permute-start.3 = (bf16[2,2,16,512]{3,2,1,0:T(8,128)(2,1)S(1)}, bf16[2,2,16,512]{3,2,1,0:T(8,128)(2,1)S(1)}, u32[]{:S(2)}, u32[]{:S(2)}) collective-permute-start(bf16[2,2,16,512]{3,2,1,0:T(8,128)(2,1)S(1)} %get-tuple-element.59), channel_id=1, source_target_pairs={{0,96},{16,112},{32,64},{48,80},{64,32},{80,48},{96,0},{112,16},{1... | collective-permute-start | bytes 196616 | tf_op jit(solution)/shard_map/ppermute | solution.py:32
  11.2 6.6 %collective-permute-start.2 = (bf16[2,2,16,512]{3,2,1,0:T(8,128)(2,1)S(1)}, bf16[2,2,16,512]{3,2,1,0:T(8,128)(2,1)S(1)}, u32[]{:S(2)}, u32[]{:S(2)}) collective-permute-start(bf16[2,2,16,512]{3,2,1,0:T(8,128)(2,1)S(1)} %get-tuple-element.59), channel_id=1, source_target_pairs={{0,64},{16,80},{32,96},{48,112},{64,0},{80,16},{96,32},{112,48},{1... | collective-permute-start | bytes 196616 | tf_op jit(solution)/shard_map/ppermute | solution.py:32
  20.4 1.6 %collective-permute-start.6 = (bf16[8,2,16,512]{3,2,1,0:T(8,128)(2,1)S(1)}, bf16[8,2,16,512]{3,2,1,0:T(8,128)(2,1)S(1)}, u32[]{:S(2)}, u32[]{:S(2)}) collective-permute-start(bf16[8,2,16,512]{3,2,1,0:T(8,128)(2,1)S(1)} %shard_map.98), channel_id=1, source_target_pairs={{0,16},{16,0},{32,48},{48,32},{64,80},{80,64},{96,112},{112,96},{1... | collective-permute-start | bytes 786440 | tf_op jit(solution)/shard_map/ppermute | solution.py:32
  25.0 3.1 %collective-permute-start.7 = (bf16[8,2,16,512]{3,2,1,0:T(8,128)(2,1)S(1)}, bf16[8,2,16,512]{3,2,1,0:T(8,128)(2,1)S(1)}, u32[]{:S(2)}, u32[]{:S(2)}) collective-permute-start(bf16[8,2,16,512]{3,2,1,0:T(8,128)(2,1)S(1)} %get-tuple-element.43), channel_id=1, source_target_pairs={{0,16},{16,0},{32,48},{48,32},{64,80},{80,64},{96,112},{112,96},{1... | collective-permute-start | bytes 786440 | tf_op jit(solution)/shard_map/ppermute | solution.py:32
  28.2 7.8 %collective-permute-start.8 = (bf16[4,2,16,512]{3,2,1,0:T(8,128)(2,1)S(1)}, bf16[4,2,16,512]{3,2,1,0:T(8,128)(2,1)S(1)}, u32[]{:S(2)}, u32[]{:S(2)}) collective-permute-start(bf16[4,2,16,512]{3,2,1,0:T(8,128)(2,1)S(1)} %shard_map.102), channel_id=1, source_target_pairs={{0,128},{16,144},{32,160},{48,176},{64,192},{80,208},{96,224},{112... | collective-permute-start | bytes 393224 | tf_op jit(solution)/shard_map/ppermute | solution.py:32
  32.1 17.0 %collective-permute-start.9 = (bf16[2,8,32,512]{3,2,1,0:T(8,128)(2,1)S(1)}, bf16[2,8,32,512]{3,2,1,0:T(8,128)(2,1)S(1)}, u32[]{:S(2)}, u32[]{:S(2)}) collective-permute-start(bf16[2,8,32,512]{3,2,1,0:T(8,128)(2,1)S(1)} %get-tuple-element.52), channel_id=1, source_target_pairs={{0,16},{16,32},{32,48},{48,64},{64,80},{80,96},{96,112},{112,128},... | collective-permute-start | bytes 1572872 | tf_op jit(solution)/shard_map/ppermute | solution.py:36
  32.2 16.9 %collective-permute-start.10 = (bf16[2,8,32,512]{3,2,1,0:T(8,128)(2,1)S(1)}, bf16[2,8,32,512]{3,2,1,0:T(8,128)(2,1)S(1)}, u32[]{:S(2)}, u32[]{:S(2)}) collective-permute-start(bf16[2,8,32,512]{3,2,1,0:T(8,128)(2,1)S(1)} %get-tuple-element.53), channel_id=1, source_target_pairs={{0,240},{16,0},{32,16},{48,32},{64,48},{80,64},{96,80},{112,96},{1... | collective-permute-start | bytes 1572872 | tf_op jit(solution)/shard_map/ppermute | solution.py:36
  40.5 8.6 %collective-permute-start.13 = (bf16[1,2,16,512]{3,2,1,0:T(8,128)(2,1)S(1)}, bf16[1,2,16,512]{3,2,1,0:T(8,128)(2,1)S(1)}, u32[]{:S(2)}, u32[]{:S(2)}) collective-permute-start(bf16[1,2,16,512]{3,2,1,0:T(8,128)(2,1)S(1)} %get-tuple-element.56), channel_id=1, source_target_pairs={{0,96},{16,112},{32,64},{48,80},{64,32},{80,48},{96,0},{112,16},{1... | collective-permute-start | bytes 98312 | tf_op jit(solution)/shard_map/ppermute | solution.py:32
  42.3 6.7 %collective-permute-start.12 = (bf16[1,2,16,512]{3,2,1,0:T(8,128)(2,1)S(1)}, bf16[1,2,16,512]{3,2,1,0:T(8,128)(2,1)S(1)}, u32[]{:S(2)}, u32[]{:S(2)}) collective-permute-start(bf16[1,2,16,512]{3,2,1,0:T(8,128)(2,1)S(1)} %get-tuple-element.57), channel_id=1, source_target_pairs={{0,64},{16,80},{32,96},{48,112},{64,0},{80,16},{96,32},{112,48},{1... | collective-permute-start | bytes 98312 | tf_op jit(solution)/shard_map/ppermute | solution.py:32
  42.3 6.7 %collective-permute-start.11 = (bf16[1,2,16,512]{3,2,1,0:T(8,128)(2,1)S(1)}, bf16[1,2,16,512]{3,2,1,0:T(8,128)(2,1)S(1)}, u32[]{:S(2)}, u32[]{:S(2)}) collective-permute-start(bf16[1,2,16,512]{3,2,1,0:T(8,128)(2,1)S(1)} %get-tuple-element.58), channel_id=1, source_target_pairs={{0,32},{16,48},{32,0},{48,16},{64,96},{80,112},{96,64},{112,80},{1... | collective-permute-start | bytes 98312 | tf_op jit(solution)/shard_map/ppermute | solution.py:32
